TPU v7x, 512 devices: a whole 4x8x8 slice. The times are simulated.
512 devices in a mesh: dp: 256 (over z, y, x), ctx: 2 (over core).
Axes of the slice: x: 4, y: 8, z: 8, core: 2. Of those that a mesh axis runs over, the one named last changes fastest.
Arguments:
- history: bfloat16 [256, 256, 512], P('dp', 'ctx'), may hold values from -6 to 6
- lengths: int32 [256], P('dp'), may hold values from 128 to 256, as said below
- input_gain: float32 [512], replicated, may hold values from 0.1 to 1.9
- gain_attn: float32 [512], replicated, may hold values from 0.1 to 1.9
- w_in: bfloat16 [512, 2048], replicated, may hold values from -0.25 to 0.25
- w_out: bfloat16 [512, 512], replicated, may hold values from -0.25 to 0.25
- cotangent: bfloat16 [256, 256, 512], P('dp', 'ctx'), may hold values from -6 to 6
Outputs:
- output: bfloat16 [256, 256, 512], P('dp', 'ctx')
- grad_history: bfloat16 [256, 256, 512], P('dp', 'ctx')
- grad_w_in: float32 [512, 2048], replicated
- grad_w_out: float32 [512, 512], replicated
- grad_gain_in: float32 [512], replicated
- grad_gain_attn: float32 [512], replicated
Inputs may be any that keep to these rules, and one draw needn't show every extreme that they name: `lengths`: each length is a multiple of 128; some user has length 256 and another 128.
All inputs are finite; a program needn't handle non-finite values.
Results may differ from a plain program's by a relative error of at most 0.0088.
Values may be sent and summed in bfloat16 or wider, within the bound.
A program may use at most 64 MiB of HBM per device.

v0:
```python
import math

import jax
import jax.numpy as jnp
from jax import lax
from jax.sharding import PartitionSpec as P

H = 8
DH = 64


EPS = 1e-05


def apply_rms_norm(tensor):
    mean = jnp.mean(tensor, axis=-1, keepdims=True)
    centered = tensor - mean
    variance = jnp.mean(centered * centered, axis=-1, keepdims=True)
    rstd = lax.rsqrt(variance + EPS)
    return (centered * rstd, rstd)


def norm_backward_pass(grad, normed, rstd):
    return rstd * (
        grad
        - jnp.mean(grad, axis=-1, keepdims=True)
        - normed * jnp.mean(grad * normed, axis=-1, keepdims=True)
    )


def silu_slope(tensor):
    sigmoid_v = jax.nn.sigmoid(tensor)
    return sigmoid_v * (1.0 + tensor * (1.0 - sigmoid_v))


def split_heads(block):
    return block.reshape(block.shape[0], H, block.shape[1] // H)


def contract_rows(left, right):
    return lax.dot_general(
        left, right, (((0,), (0,)), ((), ())), preferred_element_type=jnp.float32
    )


def contract_cols(left, right):
    return lax.dot_general(
        left, right, (((1,), (1,)), ((), ())), preferred_element_type=jnp.float32
    )


def pair_scores(query_heads, query_pos, key_heads, key_pos, length):
    scores = jnp.einsum(
        "qhd,khd->hqk", query_heads, key_heads, preferred_element_type=jnp.float32
    ) * (1.0 / math.sqrt(DH))
    pair_mask = ((key_pos[None, :] <= query_pos[:, None]) & (query_pos[:, None] < length)).astype(
        jnp.float32
    )
    return (scores, pair_mask)


def per_device(history, lengths, input_gain, gain_attn, w_in, w_out, cotangent):
    block_rows = history.shape[1]
    model_width = history.shape[2]
    score_scale = 1.0 / math.sqrt(DH)
    full_len = block_rows * lax.axis_size("ctx")
    key_step = block_rows * math.gcd(lax.axis_size("ctx"), max(1, 512 // block_rows))
    offset = lax.axis_index("ctx") * block_rows
    length = lengths[0]
    own_pos = offset + jnp.arange(block_rows, dtype=jnp.int32)
    inputs_float = history[0].astype(jnp.float32)
    standardized_input, input_inverse_deviation = apply_rms_norm(inputs_float)
    normalized_input = (standardized_input * input_gain).astype(jnp.bfloat16)
    pre_act = jnp.dot(normalized_input, w_in, preferred_element_type=jnp.float32)
    hidden = jax.nn.silu(pre_act).astype(jnp.bfloat16)
    gating = hidden[:, :model_width]
    value_rows = hidden[:, model_width : 2 * model_width]
    query_rows = hidden[:, 2 * model_width : 3 * model_width]
    key_rows = hidden[:, 3 * model_width :]
    query_heads = split_heads(query_rows)
    zero_rows = jnp.zeros((block_rows, model_width), jnp.float32)
    keys_in = lax.all_gather(key_rows, "ctx", axis=0, tiled=True)
    values_in = lax.all_gather(value_rows, "ctx", axis=0, tiled=True)
    piece_rows = keys_in.shape[0]
    sub_rows = math.gcd(piece_rows, key_step)

    def step_block(block_index, state):
        first_row = block_index * sub_rows
        key_pos = first_row + jnp.arange(sub_rows, dtype=jnp.int32)
        scores, pair_mask = pair_scores(query_heads, own_pos, split_heads(keys_in), key_pos, length)
        weights = (jax.nn.silu(scores) * pair_mask).astype(jnp.bfloat16)
        return state + jnp.einsum(
            "hqk,khd->qhd", weights, split_heads(values_in), preferred_element_type=jnp.float32
        ).reshape(block_rows, model_width)

    attended = lax.fori_loop(0, piece_rows // sub_rows, step_block, zero_rows)
    normed, rstd_attn = apply_rms_norm(attended)
    gating_f = gating.astype(jnp.float32)
    mixed = (normed * gain_attn * gating_f).astype(jnp.bfloat16)
    valid = (own_pos < length).astype(jnp.float32)[:, None]
    proj = jnp.dot(mixed, w_out, preferred_element_type=jnp.float32)
    output = (inputs_float + valid * proj).astype(jnp.bfloat16)
    cot_f = cotangent[0].astype(jnp.float32)
    d_proj = (cot_f * valid).astype(jnp.bfloat16)
    g_out = contract_rows(mixed, d_proj)
    d_mixed = contract_cols(d_proj, w_out)
    d_gating = d_mixed * normed * gain_attn
    g_attn = jnp.sum(d_mixed * normed * gating_f, axis=0)
    d_att = norm_backward_pass(d_mixed * gain_attn * gating_f, normed, rstd_attn).astype(
        jnp.bfloat16
    )
    d_att_heads = split_heads(d_att)
    back_keys, back_values = (
        lax.all_gather(key_rows, "ctx", axis=0, tiled=True),
        lax.all_gather(value_rows, "ctx", axis=0, tiled=True),
    )
    terms_init = jnp.zeros((full_len, 2 * model_width), jnp.float32)

    def query_side(block_index, state_pair):
        first_row = block_index * key_step
        key_pos = first_row + jnp.arange(key_step, dtype=jnp.int32)
        d_query, key_terms = state_pair
        key_heads = split_heads(back_keys)
        scores, pair_mask = pair_scores(query_heads, own_pos, key_heads, key_pos, length)
        pair_grads = jnp.einsum(
            "qhd,khd->hqk",
            d_att_heads,
            split_heads(back_values),
            preferred_element_type=jnp.float32,
        )
        slopes = (pair_grads * silu_slope(scores) * pair_mask).astype(jnp.bfloat16)
        d_query = (
            d_query
            + jnp.einsum(
                "hqk,khd->qhd", slopes, key_heads, preferred_element_type=jnp.float32
            ).reshape(block_rows, model_width)
            * score_scale
        )
        weights = (jax.nn.silu(scores) * pair_mask).astype(jnp.bfloat16)
        block_keys = (
            jnp.einsum(
                "hqk,qhd->khd", slopes, query_heads, preferred_element_type=jnp.float32
            ).reshape(key_step, model_width)
            * score_scale
        )
        block_values = jnp.einsum(
            "hqk,qhd->khd", weights, d_att_heads, preferred_element_type=jnp.float32
        ).reshape(key_step, model_width)
        key_terms = jnp.concatenate([block_keys, block_values], axis=1)
        return (d_query, key_terms)

    d_query, key_terms = lax.fori_loop(0, full_len // key_step, query_side, (zero_rows, terms_init))
    own_terms = lax.psum_scatter(key_terms, "ctx", scatter_dimension=0, tiled=True)
    d_keys = own_terms[:, :model_width]
    d_values = own_terms[:, model_width:]
    d_hidden = jnp.concatenate([d_gating, d_values, d_query, d_keys], axis=1)
    d_pre = (d_hidden * silu_slope(pre_act)).astype(jnp.bfloat16)
    g_in = contract_rows(normalized_input, d_pre)
    normed_gradient = contract_cols(d_pre, w_in)
    input_gain_gradient = jnp.sum(normed_gradient * standardized_input, axis=0)
    input_gradient = norm_backward_pass(
        normed_gradient * input_gain, standardized_input, input_inverse_deviation
    )
    grad_rows = (cot_f + input_gradient).astype(jnp.bfloat16)
    sums = lax.psum((g_in, g_out, input_gain_gradient, g_attn), ("dp", "ctx"))
    factor = 1.0 / math.sqrt(lax.axis_size("dp") * full_len)
    return (
        output[None],
        grad_rows[None],
        sums[0] * factor,
        sums[1] * factor,
        sums[2] * factor,
        sums[3] * factor,
    )


def solution(mesh):
    placed = (P("dp", "ctx", None), P("dp"), P(), P(), P(), P(), P("dp", "ctx", None))
    return jax.shard_map(
        per_device,
        mesh=mesh,
        in_specs=placed,
        out_specs=(P("dp", "ctx", None), P("dp", "ctx", None), P(), P(), P(), P()),
        check_vma=False,
    )
```

profile of v0, /device:TPU:1, one launch (start us, length us, event | category | flops | bytes accessed | tf_op | source)
XLA Modules:
  0.0 368.2 jit_solution(11951432041140883744)
XLA Ops:
  9.0 1.1 fusion.18
  10.7 2.4 multiply_convert_fusion.1
  13.9 8.5 %all_gather.9 = bf16[256,512]{1,0:T(8,128)(2,1)S(1)} all-gather(bf16[128,512]{1,0:T(8,128)(2,1)S(1)} %get-tuple-element.76), channel_id=1, replica_groups=mesh['dp'=256,'ctx'=2] {'ctx'}, dimensions={0}, use_global_device_ids=true | all-gather | bytes 393216 | tf_op jit(solution)/shard_map/all_gather | solution.py:82
  22.7 2.1 all_gather.8
  26.5 1.5 multiply_convert_fusion
  28.9 2.0 fusion.22
  31.0 1.1 multiply_convert_fusion.2
  32.2 2.1 fusion.42
  34.3 1.9 fusion.1
  36.3 2.1 copy.31
  39.4 2.0 copy.30
  41.4 2.3 pad_maximum_fusion
  43.7 2.0 convolution_multiply_fusion.3
  45.7 1.8 copy.32
  47.5 1.3 fusion.29
  48.8 12.1 %reduce-scatter.2.cloned.1.call-done = f32[128,1024]{1,0:T(8,128)} async-done(((f32[256,1024]{1,0:T(8,128)}), f32[128,1024]{1,0:T(8,128)}) %reduce-scatter.2.cloned.1.call-update) | async-done | bytes 524304 | tf_op jit(solution)/shard_map/reduce_scatter | solution.py:153
  62.0 1.8 fusion.5
  63.8 3.4 fusion.34
  68.2 1.5 fusion.17
  69.7 99.9 %all-reduce = (f32[512]{0:T(512)S(1)}, f32[512]{0:T(512)S(1)}) all-reduce(f32[512]{0:T(512)S(1)} %get-tuple-element.52, f32[512]{0:T(512)S(1)} %get-tuple-element.39), channel_id=1, replica_groups=mesh['dp'=256,'ctx'=2] {'dp','ctx'}, use_global_device_ids=true, to_apply=%region_12.13 | all-reduce | flops 1024 | bytes 8192 | tf_op jit(solution)/shard_map/psum | solution.py:165
  170.7 1.4 fusion.26
  172.1 183.2 %all-reduce.4.cloned.1.call-done = (f32[512,2048]{1,0:T(8,128)}, f32[512,512]{1,0:T(8,128)}) async-done(((f32[512,2048]{1,0:T(8,128)}, f32[512,512]{1,0:T(8,128)}), (f32[512,2048]{1,0:T(8,128)}, f32[512,512]{1,0:T(8,128)})) %all-reduce.4.cloned.1.call-update) | async-done | bytes 5242896 | tf_op jit(solution)/shard_map/psum | solution.py:165
  355.4 4.9 %broadcast_multiply_fusion = f32[512,2048]{1,0:T(8,128)} fusion(f32[512,2048]{1,0:T(8,128)} %get-tuple-element.57), kind=kLoop, calls=%fused_computation | loop fusion | flops 1048576 | bytes 8388608 | tf_op jit(solution)/shard_map/mul | solution.py:170
  360.3 1.1 broadcast_multiply_fusion.1
  (64 shorter events, 9.6 us)
Async XLA Ops:
  7.2 3.5 copy-start
  7.2 53.8 %reduce-scatter.2.cloned.1.call-start = ((), (), s32[]{:S(2)}) async-start(), calls=%async_computation.1 | async-start | bytes 1572864 | tf_op jit(solution)/shard_map/reduce_scatter | solution.py:153
  10.1 3.0 copy-start.16
  13.1 0.8 copy-start.8
  22.5 5.5 %copy-start.6 = (bf16[256,512]{0,1:T(8,128)(2,1)}, bf16[256,512]{0,1:T(8,128)(2,1)S(1)}, u32[]{:S(2)}) copy-start(bf16[256,512]{0,1:T(8,128)(2,1)S(1)} %copy.27) | copy-start | bytes 786436
  22.5 6.4 %copy-start.2 = (bf16[512,512]{1,0:T(8,128)(2,1)S(1)}, bf16[512,512]{1,0:T(8,128)(2,1)}, u32[]{:S(2)}) copy-start(bf16[512,512]{1,0:T(8,128)(2,1)} %param.12) | copy-start | bytes 1572868
  22.5 6.4 %copy-start.4 = (bf16[1,128,512]{2,1,0:T(8,128)(2,1)S(1)}, bf16[1,128,512]{2,1,0:T(8,128)(2,1)}, u32[]{:S(2)}) copy-start(bf16[1,128,512]{2,1,0:T(8,128)(2,1)} %param.13) | copy-start | bytes 393220
  22.5 6.4 %copy-start.14 = (f32[512]{0:T(512)S(1)}, f32[512]{0:T(512)}, u32[]{:S(2)}) copy-start(f32[512]{0:T(512)} %param.10) | copy-start | bytes 6148
  22.7 8.3 %copy-start.9 = (bf16[128,512]{0,1:T(8,128)(2,1)}, bf16[128,512]{0,1:T(8,128)(2,1)S(1)}, u32[]{:S(2)}) copy-start(bf16[128,512]{0,1:T(8,128)(2,1)S(1)} %copy.26) | copy-start | bytes 393220
  25.6 2.3 copy-start.7
  26.5 1.9 copy-start.12
  28.0 0.8 copy-start.3
  28.3 2.7 copy-start.15
  28.8 2.2 copy-start.17
  32.2 2.1 copy-start.11
  32.2 6.1 %copy-start.10 = (bf16[128,512]{0,1:T(8,128)(2,1)S(1)}, bf16[128,512]{0,1:T(8,128)(2,1)}, u32[]{:S(2)}) copy-start(bf16[128,512]{0,1:T(8,128)(2,1)} %copy-done.9) | copy-start | bytes 393220
  43.7 20.1 %copy-start.1 = (bf16[1,128,512]{2,1,0:T(8,128)(2,1)S(1)}, bf16[1,128,512]{2,1,0:T(8,128)(2,1)}, u32[]{:S(2)}) copy-start(bf16[1,128,512]{2,1,0:T(8,128)(2,1)} %param.7) | copy-start | bytes 393220
  43.7 20.1 %copy-start.13 = (f32[512]{0:T(512)S(1)}, f32[512]{0:T(512)}, u32[]{:S(2)}) copy-start(f32[512]{0:T(512)} %param.9) | copy-start | bytes 6148
  43.7 311.7 %all-reduce.4.cloned.1.call-start = ((), (), s32[]{:S(2)}) async-start(), calls=%async_computation.2 | async-start | bytes 10485760 | tf_op jit(solution)/shard_map/psum | solution.py:165
  355.4 4.9 %copy-start.5 = (f32[512,512]{1,0:T(8,128)S(1)}, f32[512,512]{1,0:T(8,128)}, u32[]{:S(2)}) copy-start(f32[512,512]{1,0:T(8,128)} %get-tuple-element.58) | copy-start | bytes 3145732
Sparse Core Ops, SparseCore 0:
  43.8 17.0 reduce-scatter.1
  67.4 287.9 all-reduce.3
where the time goes:
time: 370 us; the launch traced here: 368 us
  waiting for transfers between devices  195 us (53%)
  blocking collectives  110 us (30%)
  matrix products  20.4 us (6%)
  other arithmetic  17.2 us (5%)
  between operations  15.1 us (4%)
  local copies, waits for them, and re-layouts  9.49 us (3%)
    psum x1, waiting for transfers between devices, per_device(): sums = lax.psum((g_in, g_out, input_gain_gradient, g_attn), ('dp', 'ctx'))  183 us
    psum x1, blocking collectives, per_device(): sums = lax.psum((g_in, g_out, input_gain_gradient, g_attn), ('dp', 'ctx'))  99.9 us
    reduce_scatter x1, waiting for transfers between devices, per_device(): lax.psum_scatter(key_terms, 'ctx', scatter_dimension=0, tiled=True)  12.1 us
    all_gather x1, blocking collectives, per_device(): keys_in = lax.all_gather(key_rows, 'ctx', axis=0, tiled=True)  8.5 us
  transfers between devices with their start and end apart: 2, of which 2 were waited for; matrix products, arithmetic and copies ran while one was open for 3% of the time, Pallas kernels for 0%

commit v1 on v0

v1 whole, which is shorter than its diff:
```python
import functools
import math

import jax
import jax.numpy as jnp
from jax import lax
from jax.experimental import pallas as pl
from jax.experimental.pallas import tpu as pltpu
from jax.sharding import PartitionSpec as P

MESH = pl.DeviceIdType.MESH
F32 = jnp.float32
BF16 = jnp.bfloat16
D = 512
DH = 64
BLK = 128
SEQ = 256
HALF = 256
HEADS = 4
SIZES = (4, 8, 8)
EPS = 1e-05
SCORE_SCALE = 1.0 / math.sqrt(DH)
XYZ, XZY, YXZ, ZXY = (0, 1, 2), (0, 2, 1), (1, 0, 2), (2, 0, 1)
STREAMS = (
    (XYZ, 32),
    (XZY, 32),
    (XYZ, 16),
    (XZY, 16),
    (XYZ, 16),
    (XZY, 16),
    (YXZ, 16),
    (ZXY, 16),
)
LEVELS = 5


def dot(left, right, dims):
    return lax.dot_general(left, right, (dims, ((), ())), preferred_element_type=F32)


def rows_dot(left, right):
    return dot(left, right, ((1,), (0,)))


def cols_dot(left, right):
    return dot(left, right, ((1,), (1,)))


def sum_rows_dot(left, right):
    return dot(left, right, ((0,), (0,)))


def sigmoid(t):
    return 0.5 * jnp.tanh(0.5 * t) + 0.5


def standardize(t):
    centered = t - jnp.mean(t, axis=-1, keepdims=True)
    rstd = lax.rsqrt(jnp.mean(centered * centered, axis=-1, keepdims=True) + EPS)
    return centered * rstd, rstd


class Place:
    def __init__(self):
        self.dp = lax.axis_index("dp")
        self.core = lax.axis_index("ctx")
        self.pos = (lax.rem(self.dp, 4), lax.rem(self.dp // 4, 8), self.dp // 32)

    def device(self, axis, index):
        q = list(self.pos)
        q[axis] = index
        return ((q[2] * 8 + q[1]) * 4 + q[0], self.core)

    def partner(self):
        return (self.dp, 1 - self.core)


def wait_bytes(region, sem):
    pltpu.make_async_copy(region, region, sem).wait()


class Stream:
    def __init__(self, place, order, bufs, result, ssem, rsem, base):
        self.place, self.order, self.base = place, order, base
        self.src, self.r1, self.s1, self.r2, self.r3 = bufs
        self.res = result
        self.ssem, self.rsem = ssem, rsem
        self.n = [SIZES[a] for a in order]
        self.me = [place.pos[a] for a in order]

    def fan(self, phase, level, src, dst):
        n, me = self.n[level], self.me[level]
        for d in sorted(range(1, n), key=lambda d: -min(d, n - d)):
            k = lax.rem(me + d, n)
            pltpu.make_async_remote_copy(
                src_ref=src(k),
                dst_ref=dst,
                send_sem=self.ssem.at[self.base + phase],
                recv_sem=self.rsem.at[self.base + phase],
                device_id=self.place.device(self.order[level], k),
                device_id_type=MESH,
            ).start()

    def wait_recv(self, phase, region):
        wait_bytes(region, self.rsem.at[self.base + phase])

    def total(self, ref, n):
        acc = ref[0].astype(F32)
        for j in range(1, n):
            acc = acc + ref[j].astype(F32)
        return acc.astype(BF16)

    def scatter1(self):
        self.fan(0, 0, lambda k: self.src.at[k], self.r1.at[self.me[0]])

    def scatter2(self):
        n, me = self.n[0], self.me[0]
        self.wait_recv(0, self.r1.at[pl.ds(0, n - 1)])
        self.r1[me] = self.src[me]
        self.s1[...] = self.total(self.r1, n)
        self.fan(1, 1, lambda k: self.s1.at[k], self.r2.at[self.me[1]])

    def exchange(self):
        n, me = self.n[1], self.me[1]
        self.wait_recv(1, self.r2.at[pl.ds(0, n - 1)])
        self.r2[me] = self.s1[me]
        own = self.r3.at[self.me[2]]
        own[...] = self.total(self.r2, n)
        self.fan(2, 2, lambda k: own, own)

    def gather2(self):
        n = self.n[2]
        self.wait_recv(2, self.r3.at[pl.ds(0, n - 1)])
        own = self.res.at[self.me[0], self.me[1]]
        own[...] = self.total(self.r3, n)
        self.fan(3, 1, lambda k: own, own)

    def gather1(self):
        own = self.res.at[self.me[0]]
        self.wait_recv(3, own.at[pl.ds(0, self.n[1] - 1)])
        self.fan(4, 0, lambda k: own, own)

    def finish(self):
        self.wait_recv(4, self.res.at[pl.ds(0, self.n[0] - 1)])

    def drain(self):
        n = self.n
        regions = (
            self.r1.at[pl.ds(0, n[0] - 1)],
            self.r2.at[pl.ds(0, n[1] - 1)],
            self.r3.at[pl.ds(0, n[2] - 1)],
            self.res.at[0, pl.ds(0, n[1] - 1)],
            self.res.at[pl.ds(0, n[0] - 1)],
        )
        for phase, region in enumerate(regions):
            wait_bytes(region, self.ssem.at[self.base + phase])


def share_kernel(hist_ref, cot_ref, gain_ref, normed_ref, cots_ref, ssem, rsem):
    place = Place()
    core = place.core
    barrier = pltpu.get_barrier_semaphore()
    pl.semaphore_signal(barrier, inc=1, device_id=place.partner(), device_id_type=MESH)
    xhat, _ = standardize(hist_ref[...].astype(F32))
    normed_ref[core] = (xhat * gain_ref[...]).astype(BF16)
    cots_ref[core] = cot_ref[...]
    pl.semaphore_wait(barrier, 1)
    copies = []
    for i, ref in enumerate((cots_ref, normed_ref)):
        copies.append(
            pltpu.make_async_remote_copy(
                src_ref=ref.at[core],
                dst_ref=ref.at[core],
                send_sem=ssem.at[i],
                recv_sem=rsem.at[i],
                device_id=place.partner(),
                device_id_type=MESH,
            )
        )
        copies[-1].start()
    for copy in copies:
        copy.wait()


def layer_kernel(
    len_ref, hist_ref, normed_ref, cots_ref, gain_in_ref, gain_attn_ref, w_in_ref, w_out_ref,
    out_ref, grad_ref, gains_ref, *rest,
):
    ns = len(STREAMS)
    results, rest = rest[:ns], rest[ns:]
    stream_bufs, rest = rest[: 5 * ns], rest[5 * ns :]
    (
        w_own, wo_own, hid, slope, weights, turn, slopes, dpre, stat_own, stat_other, proj, proj_in, dnorm, dnorm_in,
        gx0, gx1, gx2, gx3,
        wsem, ssem, rsem, psem, qsem, gssem, grsem, fssem, frsem,
    ) = rest
    place = Place()
    core = place.core
    partner = place.partner()

    barrier = pltpu.get_barrier_semaphore()
    for axis, n in enumerate(SIZES):
        for d in range(1, n):
            pl.semaphore_signal(
                barrier,
                inc=1,
                device_id=place.device(axis, lax.rem(place.pos[axis] + d, n)),
                device_id_type=MESH,
            )
    pl.semaphore_signal(barrier, inc=1, device_id=partner, device_id_type=MESH)

    first = pl.multiple_of(core * HALF, HALF)
    loads = []
    for g in range(4):
        loads.append(
            pltpu.make_async_copy(
                w_in_ref.at[:, pl.ds(pl.multiple_of(g * D + first, HALF), HALF)], w_own.at[g], wsem.at[g]
            )
        )
    loads.append(pltpu.make_async_copy(w_out_ref.at[pl.ds(first, HALF), :], wo_own, wsem.at[4]))
    for load in loads:
        load.start()

    streams = [
        Stream(place, order, stream_bufs[5 * i : 5 * i + 5], results[i].at[core], ssem, rsem, LEVELS * i)
        for i, (order, _) in enumerate(STREAMS)
    ]

    def to_partner(src, dst, i):
        copy = pltpu.make_async_remote_copy(
            src_ref=src,
            dst_ref=dst,
            send_sem=psem.at[i],
            recv_sem=qsem.at[i],
            device_id=partner,
            device_id_type=MESH,
        )
        copy.start()
        return copy

    length = len_ref[0]
    row = lax.broadcasted_iota(jnp.int32, (SEQ, 1), 0)
    valid = (row < length).astype(F32)
    normed = normed_ref[...].reshape(SEQ, D)
    d_proj = (cots_ref[...].reshape(SEQ, D).astype(F32) * valid).astype(BF16)
    gain_attn = gain_attn_ref[:, pl.ds(first, HALF)]

    for g in (2, 3, 1, 0):
        loads[g].wait()
        pre = rows_dot(normed, w_own[g])
        sig = sigmoid(pre)
        hid[g] = (pre * sig).astype(BF16)
        slope[g] = sig * (1.0 + pre * (1.0 - sig))
    q_pos = lax.broadcasted_iota(jnp.int32, (SEQ, SEQ), 0)
    k_pos = lax.broadcasted_iota(jnp.int32, (SEQ, SEQ), 1)
    mask = ((k_pos <= q_pos) & (q_pos < length)).astype(F32)
    lane_head = lax.broadcasted_iota(jnp.int32, (1, HALF), 1) // DH

    def of_head(t, h):
        return jnp.where(lane_head == h, t, jnp.zeros_like(t))

    query, key, value = hid[2], hid[3], hid[1]
    attended = jnp.zeros((SEQ, HALF), F32)
    for h in range(HEADS):
        scores = cols_dot(of_head(query, h), key) * SCORE_SCALE
        sig = sigmoid(scores)
        weight = (scores * sig * mask).astype(BF16)
        weights[h] = weight
        turn[h] = sig * (1.0 + scores * (1.0 - sig)) * mask
        attended = attended + rows_dot(weight, of_head(value, h))

    loads[4].wait()
    gating = hid[0].astype(F32)
    d_mixed = cols_dot(d_proj, wo_own[...])
    g = d_mixed * gain_attn * gating
    half_mean = jnp.mean(attended, axis=-1, keepdims=True)
    centered = attended - half_mean
    half_sq = jnp.sum(centered * centered, axis=-1, keepdims=True)
    half_g = jnp.sum(g, axis=-1, keepdims=True)
    half_gc = jnp.sum(g * centered, axis=-1, keepdims=True)
    lane = lax.broadcasted_iota(jnp.int32, (SEQ, 128), 1)
    stat_own[...] = jnp.where(
        lane == 0, half_mean, jnp.where(lane == 1, half_sq, jnp.where(lane == 2, half_g, half_gc))
    )
    pl.semaphore_wait(barrier, 18)
    stat_copy = to_partner(stat_own, stat_other, 0)
    stat_copy.wait()
    other = stat_other[...]
    o_mean, o_sq, o_g, o_gc = (other[:, i : i + 1] for i in range(4))
    mean = 0.5 * (half_mean + o_mean)
    up, o_up = half_mean - mean, o_mean - mean
    var = (half_sq + o_sq + HALF * (up * up + o_up * o_up)) * (1.0 / D)
    rstd = lax.rsqrt(var + EPS)
    mean_g = (half_g + o_g) * (1.0 / D)
    mean_gn = rstd * (half_gc + o_gc + half_g * up + o_g * o_up) * (1.0 / D)
    norm = (attended - mean) * rstd
    ng = norm * gain_attn
    mixed = (ng * gating).astype(BF16)
    d_att = (rstd * (g - mean_g - norm * mean_gn)).astype(BF16)
    g_attn = jnp.sum(d_mixed * norm * gating, axis=0, keepdims=True)

    def put(stream, first_row, rows, part):
        n = streams[stream].n
        streams[stream].src[:, :, first_row : first_row + rows, :] = part.astype(BF16).reshape(n[0], n[1], rows, 128)

    def weight_grad(g, d_hidden):
        d_pre = (d_hidden * slope[g]).astype(BF16)
        dpre[g] = d_pre
        return sum_rows_dot(normed, d_pre)

    g_u = weight_grad(0, d_mixed * ng)
    g_out = sum_rows_dot(mixed, d_proj)
    for half in range(2):
        put(half, 0, 16, g_u[:, half * 128 : half * 128 + 128])
        blocks = [g_out[:, (2 * half + i) * 128 : (2 * half + i) * 128 + 128] for i in range(2)]
        put(half, 16, 16, jnp.concatenate(blocks, axis=0))
        streams[half].scatter1()

    d_values = jnp.zeros((SEQ, HALF), F32)
    for h in range(HEADS):
        d_att_h = of_head(d_att, h)
        d_values = d_values + sum_rows_dot(weights[h], d_att_h)
    g_v = weight_grad(1, d_values)
    for half in range(2):
        put(2 + half, 0, 16, g_v[:, half * 128 : half * 128 + 128])
        streams[2 + half].scatter1()

    d_query = jnp.zeros((SEQ, HALF), F32)
    d_keys = jnp.zeros((SEQ, HALF), F32)
    for h in range(HEADS):
        pair_grads = cols_dot(of_head(d_att, h), value)
        slopes_h = (pair_grads * turn[h]).astype(BF16)
        d_query = d_query + rows_dot(slopes_h, of_head(key, h))
        d_keys = d_keys + sum_rows_dot(slopes_h, of_head(query, h))
    g_q = weight_grad(2, d_query * SCORE_SCALE)
    for half in range(2):
        put(4 + half, 0, 16, g_q[:, half * 128 : half * 128 + 128])
        streams[4 + half].scatter1()
    g_k = weight_grad(3, d_keys * SCORE_SCALE)
    for half in range(2):
        put(6 + half, 0, 16, g_k[:, half * 128 : half * 128 + 128])
        streams[6 + half].scatter1()

    d_norm = cols_dot(dpre[0], w_own[0])
    for g in range(1, 4):
        d_norm = d_norm + cols_dot(dpre[g], w_own[g])
    dnorm[...] = d_norm.reshape(2, BLK, D)
    dnorm_copy = to_partner(dnorm.at[1 - core], dnorm_in, 1)
    for s in streams[:2]:
        s.scatter2()
    proj[...] = rows_dot(mixed, wo_own[...]).reshape(2, BLK, D)
    proj_copy = to_partner(proj.at[1 - core], proj_in, 2)

    history = hist_ref[...].astype(F32)
    xhat, rstd_in = standardize(history)
    dnorm_copy.wait()
    d_norm = dnorm[core] + dnorm_in[...]
    gain_part = jnp.sum(d_norm * xhat, axis=0, keepdims=True)

    mine = (core == 0).astype(F32)
    gx0_own = gx0.at[core]
    for i in range(4):
        gx0_own[i : i + 1, :] = gain_part[:, i * 128 : i * 128 + 128]
    for i in range(2):
        part = g_attn[:, i * 128 : i * 128 + 128]
        gx0_own[4 + i : 5 + i, :] = part * mine
        gx0_own[6 + i : 7 + i, :] = part * (1.0 - mine)
    gain_copy = to_partner(gx0_own, gx0_own, 3)

    def gains_fan(axis, buf):
        n, me = SIZES[axis], place.pos[axis]
        own = buf.at[me]
        for d in range(1, n):
            pltpu.make_async_remote_copy(
                src_ref=own,
                dst_ref=own,
                send_sem=gssem.at[axis],
                recv_sem=grsem.at[axis],
                device_id=place.device(axis, lax.rem(me + d, n)),
                device_id_type=MESH,
            ).start()

    def gains_total(axis, buf):
        n = SIZES[axis]
        wait_bytes(buf.at[pl.ds(0, n - 1)], grsem.at[axis])
        acc = buf[0]
        for j in range(1, n):
            acc = acc + buf[j]
        return acc

    for s in streams[2:4]:
        s.scatter2()
    gain_copy.wait()
    gx1[place.pos[0]] = gx0[0] + gx0[1]
    gains_fan(0, gx1)
    for s in streams[4:]:
        s.scatter2()

    e = d_norm * gain_in_ref[...]
    d_hist = rstd_in * (
        e - jnp.mean(e, axis=-1, keepdims=True) - xhat * jnp.mean(e * xhat, axis=-1, keepdims=True)
    )
    grad_ref[...] = (cots_ref[core].astype(F32) + d_hist).astype(BF16)
    proj_copy.wait()
    own_row = lax.broadcasted_iota(jnp.int32, (BLK, 1), 0) + core * BLK
    own_valid = (own_row < length).astype(F32)
    out_ref[...] = (history + own_valid * (proj[core] + proj_in[...])).astype(BF16)

    for s in streams[:4]:
        s.exchange()
    gx2[place.pos[1]] = gains_total(0, gx1)
    gains_fan(1, gx2)
    for s in streams[4:]:
        s.exchange()
    for s in streams[:4]:
        s.gather2()
    gx3[place.pos[2]] = gains_total(1, gx2)
    gains_fan(2, gx3)
    for s in streams[4:]:
        s.gather2()
    for s in streams:
        s.gather1()
    gains_ref[...] = gains_total(2, gx3)
    forwards = []
    for i, s in enumerate(streams):
        s.finish()
        forwards.append(
            pltpu.make_async_remote_copy(
                src_ref=s.res,
                dst_ref=s.res,
                send_sem=fssem.at[i],
                recv_sem=frsem.at[i],
                device_id=partner,
                device_id_type=MESH,
            )
        )
        forwards[-1].start()
    for axis, buf in enumerate((gx1, gx2, gx3)):
        wait_bytes(buf.at[pl.ds(0, SIZES[axis] - 1)], gssem.at[axis])
    for s in streams:
        s.drain()
    for copy in forwards:
        copy.wait()


def widen_kernel(factor, *refs):
    ns = len(STREAMS)
    gains_ref, results = refs[0], refs[1 : 1 + ns]
    w_in_ref, w_out_ref, gin_ref, gattn_ref = refs[1 + ns :]

    def wide(t):
        return t.astype(F32) * factor

    for g in range(4):
        for half in range(2):
            res = results[2 * g + half]
            for core in range(2):
                column = (4 * g + 2 * core + half) * 128
                part = res[core, :, :, 0:16, :].reshape(D, 128)
                w_in_ref[:, column : column + 128] = wide(part)
    for half in range(2):
        for core in range(2):
            part = wide(results[half][core, :, :, 16:32, :].reshape(D, 128))
            for i in range(2):
                column = (2 * half + i) * 128
                w_out_ref[core * HALF : core * HALF + HALF, column : column + 128] = part[i * HALF : i * HALF + HALF]
    for i in range(4):
        gin_ref[:, i * 128 : i * 128 + 128] = gains_ref[i : i + 1, :] * factor
        gattn_ref[:, i * 128 : i * 128 + 128] = gains_ref[4 + i : 5 + i, :] * factor


VMEM = pl.BlockSpec(memory_space=pltpu.VMEM)
SMEM = pl.BlockSpec(memory_space=pltpu.SMEM)
ANY = pl.BlockSpec(memory_space=pl.ANY)


def shape(dims, kind):
    return jax.ShapeDtypeStruct(dims, kind)


def per_device(users, history, lengths, input_gain, gain_attn, w_in, w_out, cotangent):
    history, cotangent = history[0], cotangent[0]
    input_gain, gain_attn = input_gain[None], gain_attn[None]
    dma = pltpu.SemaphoreType.DMA
    normed, cots = pl.pallas_call(
        share_kernel,
        out_shape=(shape((2, BLK, D), BF16),) * 2,
        in_specs=[VMEM] * 3,
        out_specs=(VMEM,) * 2,
        scratch_shapes=[dma((2,)), dma((2,))],
        compiler_params=pltpu.CompilerParams(collective_id=1, has_side_effects=True, vmem_limit_bytes=8 << 20),
        name="share",
    )(history, cotangent, input_gain)

    buffers, result_shapes = [], []
    for order, rows in STREAMS:
        n = [SIZES[a] for a in order]
        result_shapes.append(shape((2, n[0], n[1], rows, 128), BF16))
        buffers += [
            pltpu.VMEM((n[0], n[1], rows, 128), BF16),
            pltpu.VMEM((n[0], n[1], rows, 128), BF16),
            pltpu.VMEM((n[1], rows, 128), BF16),
            pltpu.VMEM((n[1], rows, 128), BF16),
            pltpu.VMEM((n[2], rows, 128), BF16),
        ]
    ns = len(STREAMS)
    out, grad, gains, *results = pl.pallas_call(
        layer_kernel,
        out_shape=(shape((BLK, D), BF16), shape((BLK, D), BF16), shape((8, 128), F32), *result_shapes),
        in_specs=[SMEM, VMEM, VMEM, VMEM, VMEM, VMEM, ANY, ANY],
        out_specs=(VMEM,) * (3 + ns),
        scratch_shapes=buffers
        + [
            pltpu.VMEM((4, D, HALF), BF16),
            pltpu.VMEM((HALF, D), BF16),
            pltpu.VMEM((4, SEQ, HALF), BF16),
            pltpu.VMEM((4, SEQ, HALF), F32),
            pltpu.VMEM((HEADS, SEQ, SEQ), BF16),
            pltpu.VMEM((HEADS, SEQ, SEQ), F32),
            pltpu.VMEM((HEADS, SEQ, SEQ), BF16),
            pltpu.VMEM((4, SEQ, HALF), BF16),
            pltpu.VMEM((SEQ, 128), F32),
            pltpu.VMEM((SEQ, 128), F32),
            pltpu.VMEM((2, BLK, D), F32),
            pltpu.VMEM((BLK, D), F32),
            pltpu.VMEM((2, BLK, D), F32),
            pltpu.VMEM((BLK, D), F32),
            pltpu.VMEM((2, 8, 128), F32),
            pltpu.VMEM((4, 8, 128), F32),
            pltpu.VMEM((8, 8, 128), F32),
            pltpu.VMEM((8, 8, 128), F32),
            dma((5,)),
            dma((LEVELS * ns,)),
            dma((LEVELS * ns,)),
            dma((4,)),
            dma((4,)),
            dma((3,)),
            dma((3,)),
            dma((ns,)),
            dma((ns,)),
        ],
        compiler_params=pltpu.CompilerParams(collective_id=2, has_side_effects=True, vmem_limit_bytes=48 << 20),
        name="layer",
    )(lengths, history, normed, cots, input_gain, gain_attn, w_in, w_out)

    factor = 1.0 / math.sqrt(users * SEQ)
    g_in, g_out, gain_in_grad, gain_attn_grad = pl.pallas_call(
        functools.partial(widen_kernel, factor),
        out_shape=(shape((D, 4 * D), F32), shape((D, D), F32), shape((1, D), F32), shape((1, D), F32)),
        in_specs=[VMEM] * (1 + ns),
        out_specs=(VMEM,) * 4,
        compiler_params=pltpu.CompilerParams(vmem_limit_bytes=32 << 20),
        name="widen",
    )(gains, *results)
    return out[None], grad[None], g_in, g_out, gain_in_grad[0], gain_attn_grad[0]


def solution(mesh):
    placed = (P("dp", "ctx", None), P("dp"), P(), P(), P(), P(), P("dp", "ctx", None))
    return jax.shard_map(
        functools.partial(per_device, mesh.shape["dp"]),
        mesh=mesh,
        in_specs=placed,
        out_specs=(P("dp", "ctx", None), P("dp", "ctx", None), P(), P(), P(), P()),
        check_vma=False,
    )
```

time: 370 us -> 71.2 us (0.19)
  waiting for transfers between devices: 195 us -> 0 us
  blocking collectives: 110 us -> 0 us
  Pallas kernels: 0 us -> 60.9 us
  matrix products: 20.4 us -> 0 us
  other arithmetic: 17.2 us -> 0 us
  between operations: 15.1 us -> 1.32 us
    psum x1 -> x0, waiting for transfers between devices: 183 us -> none  [per_device(): sums = lax.psum((g_in, g_out, input_gain_gradient, g_attn), ('dp', 'ctx'))]
    psum x1 -> x0, blocking collectives: 99.9 us -> none  [per_device(): sums = lax.psum((g_in, g_out, input_gain_gradient, g_attn), ('dp', 'ctx'))]
    pallas_call x0 -> x3, Pallas kernels: none -> 60.9 us  [the longest x1 49.1 us: per_device(): pl.pallas_call(layer_kernel, out_shape=(shape((BLK, D), BF16), shape((BLK...]
    dot_general x12 -> x0, matrix products: 20.4 us -> none  [the longest x2 4.76 us: contract_rows(): lax.dot_general(left, right, (((0,), (0,)), ((), ())), preferred_element_...]
    reduce_scatter x1 -> x0, waiting for transfers between devices: 12.1 us -> none  [per_device(): lax.psum_scatter(key_terms, 'ctx', scatter_dimension=0, tiled=True)]
    all_gather x2 -> x0, blocking collectives: 10.6 us -> none  [the longest x1 8.5 us: per_device(): keys_in = lax.all_gather(key_rows, 'ctx', axis=0, tiled=True)]
    unnamed x36 -> x18, local copies, waits for them, and re-layouts: 1.2 us -> 8.69 us
    mul x4 -> x0, other arithmetic: 7.1 us -> none  [the longest x1 4.88 us: per_device(): sums[0] * factor]
  transfers between devices with their start and end apart: 2 -> 0, of which waited for: 2 -> 0; matrix products, arithmetic and copies ran while one was open for 3% -> 0% of each run, Pallas kernels for 0% -> 0%
where the time goes in v1:
time: 71.2 us; the launch traced here: 70.9 us
  Pallas kernels  60.9 us (86%)
  local copies, waits for them, and re-layouts  8.69 us (12%)
  between operations  1.32 us (2%)
    pallas_call x1, Pallas kernels, per_device(): pl.pallas_call(layer_kernel, out_shape=(shape((BLK, D), BF16), shape((BLK...  49.1 us
    pallas_call x1, Pallas kernels, per_device(): pl.pallas_call(share_kernel, out_shape=(shape((2, BLK, D), BF16),) * 2, i...  8.85 us
    unnamed x18, local copies, waits for them, and re-layouts  8.69 us
    pallas_call x1, Pallas kernels, per_device(): pl.pallas_call(functools.partial(widen_kernel, factor), out_shape=(shape(...  2.89 us

profile of v1, /device:TPU:1, one launch (start us, length us, event | category | flops | bytes accessed | tf_op | source)
XLA Modules:
  0.0 70.9 jit_solution(14760344006144602010)
XLA Ops:
  1.3 0.0 copy-start.1
  1.3 0.9 %copy-done.1 = bf16[1,128,512]{2,1,0:T(8,128)(2,1)S(1)} copy-done((bf16[1,128,512]{2,1,0:T(8,128)(2,1)S(1)}, bf16[1,128,512]{2,1,0:T(8,128)(2,1)}, u32[]{:S(2)}) %copy-start.1) | copy-done | bytes 131096
  2.2 0.0 copy-start.4
  2.2 0.9 %copy-done.4 = bf16[1,128,512]{2,1,0:T(8,128)(2,1)S(1)} copy-done((bf16[1,128,512]{2,1,0:T(8,128)(2,1)S(1)}, bf16[1,128,512]{2,1,0:T(8,128)(2,1)}, u32[]{:S(2)}) %copy-start.4) | copy-done | bytes 131096
  3.1 0.0 copy-start.5
  3.1 0.7 copy-done.5
  3.8 8.8 %share.1 = (bf16[2,128,512]{2,1,0:T(8,128)(2,1)S(1)}, bf16[2,128,512]{2,1,0:T(8,128)(2,1)S(1)}) custom-call(bf16[128,512]{1,0:T(8,128)(2,1)S(1)} %bitcast.8, bf16[128,512]{1,0:T(8,128)(2,1)S(1)} %bitcast.10, f32[1,512]{1,0:T(1,128)S(1)} %bitcast.13), custom_call_target="tpu_custom_call" | custom-call | tf_op jit(solution)/shard_map/share/pallas_call | solution.py:485
  12.6 0.0 copy-start
  12.6 1.6 %copy-done = bf16[512,2048]{1,0:T(8,128)(2,1)S(1)} copy-done((bf16[512,2048]{1,0:T(8,128)(2,1)S(1)}, bf16[512,2048]{1,0:T(8,128)(2,1)}, u32[]{:S(2)}) %copy-start) | copy-done | bytes 2097176
  14.2 0.0 copy-start.2
  14.2 0.9 %copy-done.2 = bf16[1,128,512]{2,1,0:T(8,128)(2,1)S(1)} copy-done((bf16[1,128,512]{2,1,0:T(8,128)(2,1)S(1)}, bf16[1,128,512]{2,1,0:T(8,128)(2,1)}, u32[]{:S(2)}) %copy-start.2) | copy-done | bytes 131096
  15.1 0.0 copy-start.3
  15.1 1.0 %copy-done.3 = bf16[512,512]{1,0:T(8,128)(2,1)S(1)} copy-done((bf16[512,512]{1,0:T(8,128)(2,1)S(1)}, bf16[512,512]{1,0:T(8,128)(2,1)}, u32[]{:S(2)}) %copy-start.3) | copy-done | bytes 524312
  16.2 0.0 copy-start.6
  16.2 0.7 copy-done.6
  16.9 0.0 copy-start.7
  16.9 0.7 copy-done.7
  17.5 49.1 %layer.1 = (bf16[128,512]{1,0:T(8,128)(2,1)S(1)}, bf16[128,512]{1,0:T(8,128)(2,1)S(1)}, f32[8,128]{1,0:T(8,128)S(1)}, bf16[2,4,8,32,128]{4,3,2,1,0:T(8,128)(2,1)...) custom-call(s32[1]{0:T(128)S(6)} %copy.15.len_ref, ...), custom_call_target="tpu_custom_call" | custom-call | tf_op jit(solution)/shard_map/layer/pallas_call | solution.py:507
  66.7 2.9 %widen.1 = (f32[512,2048]{1,0:T(8,128)}, f32[512,512]{1,0:T(8,128)}, f32[1,512]{1,0:T(1,128)}, f32[1,512]{1,0:T(1,128)}) custom-call(f32[8,128]{1,0:T(8,128)S(1)} %get-tuple-element.27.refs_0_, bf16[2,4,8,32,128]{4,3,2,1,0:T(8,128)(2,1)S(1)} %get-tuple-element.28.refs_1_, bf16[2,4,8,32,128]{4,3,2,1,0:T(8,128)(2,1)S(1)} %get-tuple-element.29.refs_2_, ...), custom_call_target="tpu_custom_call" | custom-call | tf_op jit(solution)/shard_map/widen/pallas_call | solution.py:547
  69.6 0.7 copy.16
  70.2 0.7 copy.17
Async XLA Ops:
  1.3 0.9 %copy-start.1 = (bf16[1,128,512]{2,1,0:T(8,128)(2,1)S(1)}, bf16[1,128,512]{2,1,0:T(8,128)(2,1)}, u32[]{:S(2)}) copy-start(bf16[1,128,512]{2,1,0:T(8,128)(2,1)} %param.7) | copy-start | bytes 393220
  2.2 0.9 %copy-start.4 = (bf16[1,128,512]{2,1,0:T(8,128)(2,1)S(1)}, bf16[1,128,512]{2,1,0:T(8,128)(2,1)}, u32[]{:S(2)}) copy-start(bf16[1,128,512]{2,1,0:T(8,128)(2,1)} %param.13) | copy-start | bytes 393220
  3.1 0.7 copy-start.5
  12.6 1.6 %copy-start = (bf16[512,2048]{1,0:T(8,128)(2,1)S(1)}, bf16[512,2048]{1,0:T(8,128)(2,1)}, u32[]{:S(2)}) copy-start(bf16[512,2048]{1,0:T(8,128)(2,1)} %w_in_ref.1) | copy-start | bytes 6291460
  14.2 0.9 %copy-start.2 = (bf16[1,128,512]{2,1,0:T(8,128)(2,1)S(1)}, bf16[1,128,512]{2,1,0:T(8,128)(2,1)}, u32[]{:S(2)}) copy-start(bf16[1,128,512]{2,1,0:T(8,128)(2,1)} %param.7) | copy-start | bytes 393220
  15.1 1.0 %copy-start.3 = (bf16[512,512]{1,0:T(8,128)(2,1)S(1)}, bf16[512,512]{1,0:T(8,128)(2,1)}, u32[]{:S(2)}) copy-start(bf16[512,512]{1,0:T(8,128)(2,1)} %w_out_ref.1) | copy-start | bytes 1572868
  16.2 0.7 copy-start.6
  16.9 0.7 copy-start.7

commit v2 on v1

v2 whole, which is shorter than its diff:
```python
import functools
import math

import jax
import jax.numpy as jnp
from jax import lax
from jax.experimental import pallas as pl
from jax.experimental.pallas import tpu as pltpu
from jax.sharding import PartitionSpec as P

MESH = pl.DeviceIdType.MESH
F32 = jnp.float32
BF16 = jnp.bfloat16
D = 512
DH = 64
BLK = 128
SEQ = 256
HALF = 256
HEADS = 4
SIZES = (4, 8, 8)
EPS = 1e-05
SCORE_SCALE = 1.0 / math.sqrt(DH)
XYZ, XZY, YXZ, ZXY = (0, 1, 2), (0, 2, 1), (1, 0, 2), (2, 0, 1)
STREAMS = (
    (XYZ, 32),
    (XZY, 32),
    (XYZ, 16),
    (XZY, 16),
    (XYZ, 16),
    (XZY, 16),
    (YXZ, 16),
    (ZXY, 16),
)
LEVELS = 5


def dot(left, right, dims):
    return lax.dot_general(left, right, (dims, ((), ())), preferred_element_type=F32)


def rows_dot(left, right):
    return dot(left, right, ((1,), (0,)))


def cols_dot(left, right):
    return dot(left, right, ((1,), (1,)))


def sum_rows_dot(left, right):
    return dot(left, right, ((0,), (0,)))


def sigmoid(t):
    return 0.5 * jnp.tanh(0.5 * t) + 0.5


def standardize(t):
    centered = t - jnp.mean(t, axis=-1, keepdims=True)
    rstd = lax.rsqrt(jnp.mean(centered * centered, axis=-1, keepdims=True) + EPS)
    return centered * rstd, rstd


class Place:
    def __init__(self):
        self.dp = lax.axis_index("dp")
        self.core = lax.axis_index("ctx")
        self.pos = (lax.rem(self.dp, 4), lax.rem(self.dp // 4, 8), self.dp // 32)

    def device(self, axis, index):
        q = list(self.pos)
        q[axis] = index
        return ((q[2] * 8 + q[1]) * 4 + q[0], self.core)

    def partner(self):
        return (self.dp, 1 - self.core)


def wait_bytes(region, sem):
    pltpu.make_async_copy(region, region, sem).wait()


class Stream:
    def __init__(self, place, order, bufs, result, ssem, rsem, base):
        self.place, self.order, self.base = place, order, base
        self.src, self.r1, self.s1, self.r2, self.r3 = bufs
        self.res = result
        self.ssem, self.rsem = ssem, rsem
        self.n = [SIZES[a] for a in order]
        self.me = [place.pos[a] for a in order]

    def fan(self, phase, level, src, dst):
        n, me = self.n[level], self.me[level]
        for d in sorted(range(1, n), key=lambda d: -min(d, n - d)):
            k = lax.rem(me + d, n)
            pltpu.make_async_remote_copy(
                src_ref=src(k),
                dst_ref=dst,
                send_sem=self.ssem.at[self.base + phase],
                recv_sem=self.rsem.at[self.base + phase],
                device_id=self.place.device(self.order[level], k),
                device_id_type=MESH,
            ).start()

    def wait_recv(self, phase, region):
        wait_bytes(region, self.rsem.at[self.base + phase])

    def total(self, ref, n):
        acc = ref[0].astype(F32)
        for j in range(1, n):
            acc = acc + ref[j].astype(F32)
        return acc.astype(BF16)

    def scatter1(self):
        self.fan(0, 0, lambda k: self.src.at[k], self.r1.at[self.me[0]])

    def scatter2(self):
        n, me = self.n[0], self.me[0]
        self.wait_recv(0, self.r1.at[pl.ds(0, n - 1)])
        self.r1[me] = self.src[me]
        self.s1[...] = self.total(self.r1, n)
        self.fan(1, 1, lambda k: self.s1.at[k], self.r2.at[self.me[1]])

    def exchange(self):
        n, me = self.n[1], self.me[1]
        self.wait_recv(1, self.r2.at[pl.ds(0, n - 1)])
        self.r2[me] = self.s1[me]
        own = self.r3.at[self.me[2]]
        own[...] = self.total(self.r2, n)
        self.fan(2, 2, lambda k: own, own)

    def gather2(self):
        n = self.n[2]
        self.wait_recv(2, self.r3.at[pl.ds(0, n - 1)])
        own = self.res.at[self.me[0], self.me[1]]
        own[...] = self.total(self.r3, n)
        self.fan(3, 1, lambda k: own, own)

    def gather1(self):
        own = self.res.at[self.me[0]]
        self.wait_recv(3, own.at[pl.ds(0, self.n[1] - 1)])
        self.fan(4, 0, lambda k: own, own)

    def finish(self):
        self.wait_recv(4, self.res.at[pl.ds(0, self.n[0] - 1)])

    def drain(self):
        n = self.n
        regions = (
            self.r1.at[pl.ds(0, n[0] - 1)],
            self.r2.at[pl.ds(0, n[1] - 1)],
            self.r3.at[pl.ds(0, n[2] - 1)],
            self.res.at[0, pl.ds(0, n[1] - 1)],
            self.res.at[pl.ds(0, n[0] - 1)],
        )
        for phase, region in enumerate(regions):
            wait_bytes(region, self.ssem.at[self.base + phase])


def layer_kernel(
    len_ref, hist_hbm, cot_hbm, gain_in_hbm, gain_attn_hbm, w_in_ref, w_out_ref,
    out_ref, grad_ref, gains_ref, *rest,
):
    ns = len(STREAMS)
    results, rest = rest[:ns], rest[ns:]
    stream_bufs, rest = rest[: 5 * ns], rest[5 * ns :]
    (
        hist, gains, cots, normed, normed_t, xhat_own, w_own, wo_own, hid, slope, q_heads, k_heads, v_heads, d_heads,
        weights, turn, attended, dpre, stat_own, stat_other, proj, proj_in, dnorm, dnorm_in, gx0, gx1, gx2, gx3,
        lsem, ssem, rsem, psem, qsem, gssem, grsem, fssem, frsem,
    ) = rest
    place = Place()
    core = place.core
    away = 1 - core
    partner = place.partner()

    with jax.named_scope("start"):
        first = pl.multiple_of(core * HALF, HALF)
        loads = [
            pltpu.make_async_copy(hist_hbm, hist, lsem.at[0]),
            pltpu.make_async_copy(gain_in_hbm, gains.at[0], lsem.at[1]),
            pltpu.make_async_copy(cot_hbm, cots.at[core], lsem.at[2]),
        ]
        w_loads = [None] * 4
        for i, g in enumerate((2, 3, 1, 0)):
            columns = pl.ds(pl.multiple_of(g * D + first, HALF), HALF)
            w_loads[g] = pltpu.make_async_copy(w_in_ref.at[:, columns], w_own.at[g], lsem.at[3 + i])
            loads.append(w_loads[g])
        wo_load = pltpu.make_async_copy(w_out_ref.at[pl.ds(first, HALF), :], wo_own, lsem.at[7])
        ga_load = pltpu.make_async_copy(gain_attn_hbm, gains.at[1], lsem.at[8])
        loads += [wo_load, ga_load]
        for load in loads:
            load.start()

        barrier = pltpu.get_barrier_semaphore()
        pl.semaphore_signal(barrier, inc=1, device_id=partner, device_id_type=MESH)
        for axis, n in enumerate(SIZES):
            for d in range(1, n):
                pl.semaphore_signal(
                    barrier,
                    inc=1,
                    device_id=place.device(axis, lax.rem(place.pos[axis] + d, n)),
                    device_id_type=MESH,
                )

    streams = [
        Stream(place, order, stream_bufs[5 * i : 5 * i + 5], results[i].at[core], ssem, rsem, LEVELS * i)
        for i, (order, _) in enumerate(STREAMS)
    ]

    def to_partner(src, dst, i):
        copy = pltpu.make_async_remote_copy(
            src_ref=src,
            dst_ref=dst,
            send_sem=psem.at[i],
            recv_sem=qsem.at[i],
            device_id=partner,
            device_id_type=MESH,
        )
        copy.start()
        return copy

    length = len_ref[0]
    lane_head = lax.broadcasted_iota(jnp.int32, (1, HALF), 1) // DH

    def valid_rows(block):
        row = lax.broadcasted_iota(jnp.int32, (BLK, 1), 0) + block * BLK
        return (row < length).astype(F32)

    def put_heads(ref, block, t):
        for h in range(HEADS):
            ref[block, h * BLK : h * BLK + BLK, :] = jnp.where(lane_head == h, t, jnp.zeros_like(t))

    def heads_beside(t):
        return jnp.concatenate([t[h * BLK : h * BLK + BLK] for h in range(HEADS)], axis=1)

    def project(block, wait):
        for g in (2, 3, 1, 0):
            if wait:
                w_loads[g].wait()
            half = 0.5 * rows_dot(normed[block], w_own[g])
            t = jnp.tanh(half)
            u = half * t
            hidden = (half + u).astype(BF16)
            slope[g, block] = (0.03125 if g == 2 else 0.5) * ((1.0 + t) * (1.0 + half - u))
            if g == 2:
                put_heads(q_heads, block, hidden * (0.5 * SCORE_SCALE))
            else:
                hid[g, block] = hidden
                if g == 3:
                    put_heads(k_heads, block, hidden)
                if g == 1:
                    put_heads(v_heads, block, hidden)

    def attend(tile, q_block, k_block, diagonal):
        half = cols_dot(q_heads[q_block], hid[3, k_block])
        t = jnp.tanh(half)
        u = half * t
        weight = half + u
        turned = (1.0 + t) * (1.0 + half - u)
        if diagonal:
            q_pos = lax.broadcasted_iota(jnp.int32, (HEADS * BLK, BLK), 0) & (BLK - 1)
            k_pos = lax.broadcasted_iota(jnp.int32, (HEADS * BLK, BLK), 1)
            allowed = k_pos <= q_pos
            weight = jnp.where(allowed, weight, 0.0)
            turned = jnp.where(allowed, turned, 0.0)
        weight = weight.astype(BF16)
        weights[tile] = weight
        turn[tile] = turned
        return rows_dot(heads_beside(weight), v_heads[k_block])

    with jax.named_scope("own_project"):
        loads[0].wait()
        loads[1].wait()
        xhat, rstd_in = standardize(hist[...].astype(F32))
        xhat_own[...] = xhat
        normed[core] = (xhat * gains[0]).astype(BF16)
        project(core, True)
    with jax.named_scope("barrier"):
        loads[2].wait()
        pl.semaphore_wait(barrier, 18)
        normed_copy = to_partner(normed.at[core], normed.at[core], 0)
        cots_copy = to_partner(cots.at[core], cots.at[core], 1)
    with jax.named_scope("own_attend"):
        attended[core] = attend(core, core, core, True)
    with jax.named_scope("share_wait"):
        normed_copy.wait_recv()
    with jax.named_scope("other_project"):
        project(away, False)
    with jax.named_scope("other_attend"):
        attended[away] = attend(away, away, away, True)
        attended[1] = attended[1] + attend(2, 1, 0, False)
    with jax.named_scope("d_mixed"):
        cots_copy.wait_recv()
        wo_load.wait()
        ga_load.wait()
        valid = jnp.concatenate([valid_rows(0), valid_rows(1)], axis=0)
        d_proj = (cots[...].reshape(SEQ, D).astype(F32) * valid).astype(BF16)
        gain_attn = gains[1, :, pl.ds(first, HALF)]
        att = attended[...].reshape(SEQ, HALF) * valid
        gating = hid[0].reshape(SEQ, HALF).astype(F32)
        d_mixed = cols_dot(d_proj, wo_own[...])
        g = d_mixed * gain_attn * gating
    with jax.named_scope("stats"):
        half_mean = jnp.mean(att, axis=-1, keepdims=True)
        centered = att - half_mean
        half_sq = jnp.sum(centered * centered, axis=-1, keepdims=True)
        half_g = jnp.sum(g, axis=-1, keepdims=True)
        half_gc = jnp.sum(g * centered, axis=-1, keepdims=True)
        lane = lax.broadcasted_iota(jnp.int32, (SEQ, 128), 1)
        stat_own[...] = jnp.where(
            lane == 0, half_mean, jnp.where(lane == 1, half_sq, jnp.where(lane == 2, half_g, half_gc))
        )
        stat_copy = to_partner(stat_own, stat_other, 2)
        normed_t[...] = normed[...].reshape(SEQ, D).T
    with jax.named_scope("stats_wait"):
        stat_copy.wait_recv()
    with jax.named_scope("norm"):
        other = stat_other[...]
        o_mean, o_sq, o_g, o_gc = (other[:, i : i + 1] for i in range(4))
        mean = 0.5 * (half_mean + o_mean)
        up, o_up = half_mean - mean, o_mean - mean
        var = (half_sq + o_sq + HALF * (up * up + o_up * o_up)) * (1.0 / D)
        rstd = lax.rsqrt(var + EPS)
        mean_g = (half_g + o_g) * (1.0 / D)
        mean_gn = rstd * (half_gc + o_gc + half_g * up + o_g * o_up) * (1.0 / D)
        norm = (att - mean) * rstd
        ng = norm * gain_attn
        mixed = (ng * gating).astype(BF16)
        d_att = (rstd * (g - mean_g - norm * mean_gn) * valid).astype(BF16)
        g_attn = jnp.sum(d_mixed * norm * gating, axis=0, keepdims=True)

    def put(stream, first_row, rows, part):
        n = streams[stream].n
        streams[stream].src[:, :, first_row : first_row + rows, :] = part.astype(BF16).reshape(n[0], n[1], rows, 128)

    def weight_grad(g, d_hidden):
        d_pre = (d_hidden * slope[g].reshape(SEQ, HALF)).astype(BF16)
        dpre[g] = d_pre
        return rows_dot(normed_t[...], d_pre)

    with jax.named_scope("grads_u"):
        g_u = weight_grad(0, d_mixed * ng)
        g_out = rows_dot(mixed.T, d_proj)
        for half in range(2):
            put(half, 0, 16, g_u[:, half * 128 : half * 128 + 128])
            blocks = [g_out[:, (2 * half + i) * 128 : (2 * half + i) * 128 + 128] for i in range(2)]
            put(half, 16, 16, jnp.concatenate(blocks, axis=0))
            streams[half].scatter1()
    with jax.named_scope("grads_v"):
        for block in range(2):
            put_heads(d_heads, block, d_att[block * BLK : block * BLK + BLK])
        d_values_0 = sum_rows_dot(weights[0], d_heads[0]) + sum_rows_dot(weights[2], d_heads[1])
        d_values_1 = sum_rows_dot(weights[1], d_heads[1])
        g_v = weight_grad(1, jnp.concatenate([d_values_0, d_values_1], axis=0))
        for half in range(2):
            put(2 + half, 0, 16, g_v[:, half * 128 : half * 128 + 128])
            streams[2 + half].scatter1()
    with jax.named_scope("grads_k"):
        slopes = []
        for tile, (q_block, k_block) in enumerate(((0, 0), (1, 1), (1, 0))):
            slopes.append((cols_dot(d_heads[q_block], hid[1, k_block]) * turn[tile]).astype(BF16))
        d_keys_0 = sum_rows_dot(slopes[0], q_heads[0]) + sum_rows_dot(slopes[2], q_heads[1])
        d_keys_1 = sum_rows_dot(slopes[1], q_heads[1])
        g_k = weight_grad(3, jnp.concatenate([d_keys_0, d_keys_1], axis=0))
        for half in range(2):
            put(6 + half, 0, 16, g_k[:, half * 128 : half * 128 + 128])
            streams[6 + half].scatter1()
    with jax.named_scope("grads_q"):
        d_query_0 = rows_dot(heads_beside(slopes[0]), k_heads[0])
        d_query_1 = rows_dot(heads_beside(slopes[1]), k_heads[1]) + rows_dot(heads_beside(slopes[2]), k_heads[0])
        g_q = weight_grad(2, jnp.concatenate([d_query_0, d_query_1], axis=0))
        for half in range(2):
            put(4 + half, 0, 16, g_q[:, half * 128 : half * 128 + 128])
            streams[4 + half].scatter1()
    with jax.named_scope("scatter2_u"):
        for s in streams[:2]:
            s.scatter2()
    with jax.named_scope("d_norm"):
        d_norm = cols_dot(dpre[0], w_own[0])
        for g in range(1, 4):
            d_norm = d_norm + cols_dot(dpre[g], w_own[g])
        dnorm[...] = d_norm.reshape(2, BLK, D)
        dnorm_copy = to_partner(dnorm.at[away], dnorm_in, 3)
    with jax.named_scope("scatter2_v"):
        for s in streams[2:4]:
            s.scatter2()
    with jax.named_scope("proj"):
        proj[...] = rows_dot(mixed, wo_own[...]).reshape(2, BLK, D)
        proj_copy = to_partner(proj.at[away], proj_in, 4)

    with jax.named_scope("gain_sums"):
        xhat = xhat_own[...]
        dnorm_copy.wait_recv()
        d_norm = dnorm[core] + dnorm_in[...]
        gain_part = jnp.sum(d_norm * xhat, axis=0, keepdims=True)
        mine = (core == 0).astype(F32)
        gx0_own = gx0.at[core]
        for i in range(4):
            gx0_own[i : i + 1, :] = gain_part[:, i * 128 : i * 128 + 128]
        for i in range(2):
            part = g_attn[:, i * 128 : i * 128 + 128]
            gx0_own[4 + i : 5 + i, :] = part * mine
            gx0_own[6 + i : 7 + i, :] = part * (1.0 - mine)
        gain_copy = to_partner(gx0_own, gx0_own, 5)

    def gains_fan(axis, buf):
        n, me = SIZES[axis], place.pos[axis]
        own = buf.at[me]
        for d in range(1, n):
            pltpu.make_async_remote_copy(
                src_ref=own,
                dst_ref=own,
                send_sem=gssem.at[axis],
                recv_sem=grsem.at[axis],
                device_id=place.device(axis, lax.rem(me + d, n)),
                device_id_type=MESH,
            ).start()

    def gains_total(axis, buf):
        n = SIZES[axis]
        wait_bytes(buf.at[pl.ds(0, n - 1)], grsem.at[axis])
        acc = buf[0]
        for j in range(1, n):
            acc = acc + buf[j]
        return acc

    with jax.named_scope("scatter2_k"):
        for s in streams[6:]:
            s.scatter2()
    with jax.named_scope("scatter2_q"):
        for s in streams[4:6]:
            s.scatter2()
    with jax.named_scope("gains_x"):
        gain_copy.wait_recv()
        gx1[place.pos[0]] = gx0[0] + gx0[1]
        gains_fan(0, gx1)

    with jax.named_scope("grad_history"):
        e = d_norm * gains[0]
        d_hist = rstd_in * (
            e - jnp.mean(e, axis=-1, keepdims=True) - xhat * jnp.mean(e * xhat, axis=-1, keepdims=True)
        )
        grad_ref[...] = (cots[core].astype(F32) + d_hist).astype(BF16)
        proj_copy.wait_recv()
        out_ref[...] = (hist[...].astype(F32) + valid_rows(core) * (proj[core] + proj_in[...])).astype(BF16)

    with jax.named_scope("exchange_uv"):
        for s in streams[:4]:
            s.exchange()
    with jax.named_scope("gains_y"):
        gx2[place.pos[1]] = gains_total(0, gx1)
        gains_fan(1, gx2)
    with jax.named_scope("exchange_qk"):
        for s in streams[4:]:
            s.exchange()
    with jax.named_scope("gather2_uv"):
        for s in streams[:4]:
            s.gather2()
    with jax.named_scope("gains_z"):
        gx3[place.pos[2]] = gains_total(1, gx2)
        gains_fan(2, gx3)
    with jax.named_scope("gather2_qk"):
        for s in streams[4:]:
            s.gather2()
    with jax.named_scope("gather1_uv"):
        for s in streams[:4]:
            s.gather1()
    with jax.named_scope("gather1_qk"):
        for s in streams[4:]:
            s.gather1()
    with jax.named_scope("gains_end"):
        gains_ref[...] = gains_total(2, gx3)
    with jax.named_scope("finish"):
        forwards = []
        for i, s in enumerate(streams):
            s.finish()
            forwards.append(
                pltpu.make_async_remote_copy(
                    src_ref=s.res,
                    dst_ref=s.res,
                    send_sem=fssem.at[i],
                    recv_sem=frsem.at[i],
                    device_id=partner,
                    device_id_type=MESH,
                )
            )
            forwards[-1].start()
    with jax.named_scope("drain"):
        for axis, buf in enumerate((gx1, gx2, gx3)):
            wait_bytes(buf.at[pl.ds(0, SIZES[axis] - 1)], gssem.at[axis])
        for copy in (normed_copy, cots_copy, stat_copy, dnorm_copy, proj_copy, gain_copy):
            copy.wait_send()
        for s in streams:
            s.drain()
        for copy in forwards:
            copy.wait()


def widen_kernel(factor, *refs):
    ns = len(STREAMS)
    out_in, grad_in, gains_ref, results = refs[0], refs[1], refs[2], refs[3 : 3 + ns]
    out_ref, grad_ref, w_in_ref, w_out_ref, gin_ref, gattn_ref, w_in_wide, w_out_wide, gains_wide, sem = refs[3 + ns :]
    copies = []

    def send(src, dst):
        copies.append(pltpu.make_async_copy(src, dst, sem.at[len(copies)]))
        copies[-1].start()

    def wide(t):
        return t.astype(F32) * factor

    for half in range(2):
        for core in range(2):
            part = wide(results[half][core, :, :, 16:32, :].reshape(D, 128))
            for i in range(2):
                column = (2 * half + i) * 128
                w_out_wide[core * HALF : core * HALF + HALF, column : column + 128] = part[i * HALF : i * HALF + HALF]
    send(w_out_wide, w_out_ref)
    for g in range(4):
        for core in range(2):
            for half in range(2):
                column = (4 * g + 2 * core + half) * 128
                part = results[2 * g + half][core, :, :, 0:16, :].reshape(D, 128)
                w_in_wide[:, column : column + 128] = wide(part)
            columns = slice((4 * g + 2 * core) * 128, (4 * g + 2 * core + 2) * 128)
            send(w_in_wide.at[:, columns], w_in_ref.at[:, columns])
    for i in range(4):
        gains_wide[0, :, i * 128 : i * 128 + 128] = gains_ref[i : i + 1, :] * factor
        gains_wide[1, :, i * 128 : i * 128 + 128] = gains_ref[4 + i : 5 + i, :] * factor
    send(gains_wide.at[0], gin_ref)
    send(gains_wide.at[1], gattn_ref)
    send(out_in, out_ref)
    send(grad_in, grad_ref)
    for copy in copies:
        copy.wait()


VMEM = pl.BlockSpec(memory_space=pltpu.VMEM)
SMEM = pl.BlockSpec(memory_space=pltpu.SMEM)
HBM = pl.BlockSpec(memory_space=pltpu.HBM)


def shape(dims, kind):
    return jax.ShapeDtypeStruct(dims, kind)


def per_device(users, history, lengths, input_gain, gain_attn, w_in, w_out, cotangent):
    history, cotangent = history[0], cotangent[0]
    input_gain, gain_attn = input_gain[None], gain_attn[None]
    operands = [history, cotangent, input_gain, gain_attn, w_in, w_out]
    operands = [pltpu.with_memory_space_constraint(t, pltpu.HBM) for t in operands]
    dma = pltpu.SemaphoreType.DMA

    buffers, result_shapes = [], []
    for order, rows in STREAMS:
        n = [SIZES[a] for a in order]
        result_shapes.append(shape((2, n[0], n[1], rows, 128), BF16))
        buffers += [
            pltpu.VMEM((n[0], n[1], rows, 128), BF16),
            pltpu.VMEM((n[0], n[1], rows, 128), BF16),
            pltpu.VMEM((n[1], rows, 128), BF16),
            pltpu.VMEM((n[1], rows, 128), BF16),
            pltpu.VMEM((n[2], rows, 128), BF16),
        ]
    ns = len(STREAMS)
    heads = pltpu.VMEM((2, HEADS * BLK, HALF), BF16)
    out, grad, gains, *results = pl.pallas_call(
        layer_kernel,
        out_shape=(shape((BLK, D), BF16), shape((BLK, D), BF16), shape((8, 128), F32), *result_shapes),
        in_specs=[SMEM] + [HBM] * 6,
        out_specs=(VMEM,) * (3 + ns),
        scratch_shapes=buffers
        + [
            pltpu.VMEM((BLK, D), BF16),
            pltpu.VMEM((2, 1, D), F32),
            pltpu.VMEM((2, BLK, D), BF16),
            pltpu.VMEM((2, BLK, D), BF16),
            pltpu.VMEM((D, SEQ), BF16),
            pltpu.VMEM((BLK, D), F32),
            pltpu.VMEM((4, D, HALF), BF16),
            pltpu.VMEM((HALF, D), BF16),
            pltpu.VMEM((4, 2, BLK, HALF), BF16),
            pltpu.VMEM((4, 2, BLK, HALF), F32),
            heads,
            heads,
            heads,
            heads,
            pltpu.VMEM((3, HEADS * BLK, BLK), BF16),
            pltpu.VMEM((3, HEADS * BLK, BLK), F32),
            pltpu.VMEM((2, BLK, HALF), F32),
            pltpu.VMEM((4, SEQ, HALF), BF16),
            pltpu.VMEM((SEQ, 128), F32),
            pltpu.VMEM((SEQ, 128), F32),
            pltpu.VMEM((2, BLK, D), F32),
            pltpu.VMEM((BLK, D), F32),
            pltpu.VMEM((2, BLK, D), F32),
            pltpu.VMEM((BLK, D), F32),
            pltpu.VMEM((2, 8, 128), F32),
            pltpu.VMEM((4, 8, 128), F32),
            pltpu.VMEM((8, 8, 128), F32),
            pltpu.VMEM((8, 8, 128), F32),
            dma((9,)),
            dma((LEVELS * ns,)),
            dma((LEVELS * ns,)),
            dma((6,)),
            dma((6,)),
            dma((3,)),
            dma((3,)),
            dma((ns,)),
            dma((ns,)),
        ],
        compiler_params=pltpu.CompilerParams(collective_id=1, has_side_effects=True, vmem_limit_bytes=48 << 20),
        name="layer",
    )(lengths, *operands)

    factor = 1.0 / math.sqrt(users * SEQ)
    out, grad, g_in, g_out, gain_in_grad, gain_attn_grad = pl.pallas_call(
        functools.partial(widen_kernel, factor),
        out_shape=(
            shape((BLK, D), BF16),
            shape((BLK, D), BF16),
            shape((D, 4 * D), F32),
            shape((D, D), F32),
            shape((1, D), F32),
            shape((1, D), F32),
        ),
        in_specs=[VMEM] * (3 + ns),
        out_specs=(HBM,) * 6,
        scratch_shapes=[
            pltpu.VMEM((D, 4 * D), F32),
            pltpu.VMEM((D, D), F32),
            pltpu.VMEM((2, 1, D), F32),
            dma((13,)),
        ],
        compiler_params=pltpu.CompilerParams(vmem_limit_bytes=32 << 20),
        name="widen",
    )(out, grad, gains, *results)
    return out[None], grad[None], g_in, g_out, gain_in_grad[0], gain_attn_grad[0]


def solution(mesh):
    placed = (P("dp", "ctx", None), P("dp"), P(), P(), P(), P(), P("dp", "ctx", None))
    return jax.shard_map(
        functools.partial(per_device, mesh.shape["dp"]),
        mesh=mesh,
        in_specs=placed,
        out_specs=(P("dp", "ctx", None), P("dp", "ctx", None), P(), P(), P(), P()),
        check_vma=False,
    )
```

time: 71.2 us -> 61.7 us (0.87)
  local copies, waits for them, and re-layouts: 8.69 us -> 0 us
    pallas_call x1 -> x0, Pallas kernels: 8.85 us -> none  [per_device(): pl.pallas_call(share_kernel, out_shape=(shape((2, BLK, D), BF16),) * 2, i...]
    unnamed x18 -> x0, local copies, waits for them, and re-layouts: 8.69 us -> none
    pallas_call x1, Pallas kernels: 49.1 us -> 57.6 us  [per_device(): pl.pallas_call(layer_kernel, out_shape=(shape((BLK, D), BF16), shape((BLK...]
where the time goes in v2:
time: 61.7 us; the launch traced here: 61.5 us
  Pallas kernels  60.2 us (98%)
  between operations  1.29 us (2%)
    pallas_call x1, Pallas kernels, per_device(): pl.pallas_call(layer_kernel, out_shape=(shape((BLK, D), BF16), shape((BLK...  57.6 us
    pallas_call x1, Pallas kernels, per_device(): pl.pallas_call(functools.partial(widen_kernel, factor), out_shape=(shape(...  2.64 us

profile of v2, /device:TPU:1, one launch (start us, length us, event | category | flops | bytes accessed | tf_op | source)
XLA Modules:
  0.0 61.5 jit_solution(17061968982713409290)
XLA Ops:
  1.3 57.6 %layer.1 = (bf16[128,512]{1,0:T(8,128)(2,1)S(1)}, bf16[128,512]{1,0:T(8,128)(2,1)S(1)}, f32[8,128]{1,0:T(8,128)S(1)}, bf16[2,4,8,32,128]{4,3,2,1,0:T(8,128)(2,1)...) custom-call(s32[1]{0:T(128)S(6)} %copy.13.len_ref, ...), custom_call_target="tpu_custom_call" | custom-call | tf_op jit(solution)/shard_map/layer/pallas_call | solution.py:567
  58.9 2.6 %widen.1 = (bf16[128,512]{1,0:T(8,128)(2,1)}, bf16[128,512]{1,0:T(8,128)(2,1)}, f32[512,2048]{1,0:T(8,128)}, f32[512,512]{1,0:T(8,128)}, f32[1,512]{1,0:T(1,128)}, /*index=5*/f32[1,512]{1,0:T(1,128)}) custom-call(bf16[128,512]{1,0:T(8,128)(2,1)S(1)} %get-tuple-element.23.refs_0_, bf16[128,512]{1,0:T(8,128)(2,1)S(1)} %get-tuple-element.24.refs_1_, ...), custom_call_target="tpu_custom_call" | custom-call | tf_op jit(solution)/shard_map/widen/pallas_call | solution.py:617

commit v3 on v2

--- a/solution.py
+++ b/solution.py
@@ -21,16 +21,10 @@
 EPS = 1e-05
 SCORE_SCALE = 1.0 / math.sqrt(DH)
 XYZ, XZY, YXZ, ZXY = (0, 1, 2), (0, 2, 1), (1, 0, 2), (2, 0, 1)
-STREAMS = (
-    (XYZ, 32),
-    (XZY, 32),
-    (XYZ, 16),
-    (XZY, 16),
-    (XYZ, 16),
-    (XZY, 16),
-    (YXZ, 16),
-    (ZXY, 16),
-)
+ROWS = 16
+STREAMS = (XYZ, XZY, YXZ, ZXY, YXZ, ZXY, XYZ, XZY, XYZ, XZY)
+GATING, OUT, VALUES, KEYS, QUERIES = 0, 2, 4, 6, 8
+STREAM_OF = (GATING, VALUES, QUERIES, KEYS)
 LEVELS = 5
 
 
@@ -65,14 +59,12 @@
         self.dp = lax.axis_index("dp")
         self.core = lax.axis_index("ctx")
         self.pos = (lax.rem(self.dp, 4), lax.rem(self.dp // 4, 8), self.dp // 32)
-
-    def device(self, axis, index):
-        q = list(self.pos)
-        q[axis] = index
-        return ((q[2] * 8 + q[1]) * 4 + q[0], self.core)
-
-    def partner(self):
-        return (self.dp, 1 - self.core)
+        self.partner = (self.dp, 1 - self.core)
+        self.peers = []
+        for axis, (n, stride) in enumerate(zip(SIZES, (1, 4, 32))):
+            me = self.pos[axis]
+            others = [lax.rem(me + d, n) for d in sorted(range(1, n), key=lambda d: -min(d, n - d))]
+            self.peers.append([(k, (self.dp + (k - me) * stride, self.core)) for k in others])
 
 
 def wait_bytes(region, sem):
@@ -89,15 +81,13 @@
         self.me = [place.pos[a] for a in order]
 
     def fan(self, phase, level, src, dst):
-        n, me = self.n[level], self.me[level]
-        for d in sorted(range(1, n), key=lambda d: -min(d, n - d)):
-            k = lax.rem(me + d, n)
+        for k, device in self.place.peers[self.order[level]]:
             pltpu.make_async_remote_copy(
                 src_ref=src(k),
                 dst_ref=dst,
                 send_sem=self.ssem.at[self.base + phase],
                 recv_sem=self.rsem.at[self.base + phase],
-                device_id=self.place.device(self.order[level], k),
+                device_id=device,
                 device_id_type=MESH,
             ).start()
 
@@ -171,7 +161,7 @@
     place = Place()
     core = place.core
     away = 1 - core
-    partner = place.partner()
+    partner = place.partner
 
     with jax.named_scope("start"):
         first = pl.multiple_of(core * HALF, HALF)
@@ -193,18 +183,13 @@
 
         barrier = pltpu.get_barrier_semaphore()
         pl.semaphore_signal(barrier, inc=1, device_id=partner, device_id_type=MESH)
-        for axis, n in enumerate(SIZES):
-            for d in range(1, n):
-                pl.semaphore_signal(
-                    barrier,
-                    inc=1,
-                    device_id=place.device(axis, lax.rem(place.pos[axis] + d, n)),
-                    device_id_type=MESH,
-                )
+        for peers in place.peers:
+            for _, device in peers:
+                pl.semaphore_signal(barrier, inc=1, device_id=device, device_id_type=MESH)
 
     streams = [
         Stream(place, order, stream_bufs[5 * i : 5 * i + 5], results[i].at[core], ssem, rsem, LEVELS * i)
-        for i, (order, _) in enumerate(STREAMS)
+        for i, order in enumerate(STREAMS)
     ]
 
     def to_partner(src, dst, i):
@@ -219,12 +204,11 @@
         copy.start()
         return copy
 
-    length = len_ref[0]
     lane_head = lax.broadcasted_iota(jnp.int32, (1, HALF), 1) // DH
 
     def valid_rows(block):
         row = lax.broadcasted_iota(jnp.int32, (BLK, 1), 0) + block * BLK
-        return (row < length).astype(F32)
+        return (row < len_ref[0]).astype(F32)
 
     def put_heads(ref, block, t):
         for h in range(HEADS):
@@ -329,9 +313,17 @@
         d_att = (rstd * (g - mean_g - norm * mean_gn) * valid).astype(BF16)
         g_attn = jnp.sum(d_mixed * norm * gating, axis=0, keepdims=True)
 
-    def put(stream, first_row, rows, part):
-        n = streams[stream].n
-        streams[stream].src[:, :, first_row : first_row + rows, :] = part.astype(BF16).reshape(n[0], n[1], rows, 128)
+    def put(group, halves):
+        for half, part in enumerate(halves):
+            stream = streams[group + half]
+            stream.src[...] = part.astype(BF16).reshape(stream.n[0], stream.n[1], ROWS, 128)
+            stream.scatter1()
+
+    def columns_in_halves(t):
+        return [t[:, :128], t[:, 128:]]
+
+    def of(group):
+        return streams[group : group + 2]
 
     def weight_grad(g, d_hidden):
         d_pre = (d_hidden * slope[g].reshape(SEQ, HALF)).astype(BF16)
@@ -339,41 +331,29 @@
         return rows_dot(normed_t[...], d_pre)
 
     with jax.named_scope("grads_u"):
-        g_u = weight_grad(0, d_mixed * ng)
+        put(GATING, columns_in_halves(weight_grad(0, d_mixed * ng)))
         g_out = rows_dot(mixed.T, d_proj)
-        for half in range(2):
-            put(half, 0, 16, g_u[:, half * 128 : half * 128 + 128])
-            blocks = [g_out[:, (2 * half + i) * 128 : (2 * half + i) * 128 + 128] for i in range(2)]
-            put(half, 16, 16, jnp.concatenate(blocks, axis=0))
-            streams[half].scatter1()
+        g_out = [g_out[:, i * 128 : i * 128 + 128] for i in range(4)]
+        put(OUT, [jnp.concatenate(g_out[:2], axis=0), jnp.concatenate(g_out[2:], axis=0)])
     with jax.named_scope("grads_v"):
         for block in range(2):
             put_heads(d_heads, block, d_att[block * BLK : block * BLK + BLK])
         d_values_0 = sum_rows_dot(weights[0], d_heads[0]) + sum_rows_dot(weights[2], d_heads[1])
         d_values_1 = sum_rows_dot(weights[1], d_heads[1])
-        g_v = weight_grad(1, jnp.concatenate([d_values_0, d_values_1], axis=0))
-        for half in range(2):
-            put(2 + half, 0, 16, g_v[:, half * 128 : half * 128 + 128])
-            streams[2 + half].scatter1()
+        put(VALUES, columns_in_halves(weight_grad(1, jnp.concatenate([d_values_0, d_values_1], axis=0))))
     with jax.named_scope("grads_k"):
         slopes = []
         for tile, (q_block, k_block) in enumerate(((0, 0), (1, 1), (1, 0))):
             slopes.append((cols_dot(d_heads[q_block], hid[1, k_block]) * turn[tile]).astype(BF16))
         d_keys_0 = sum_rows_dot(slopes[0], q_heads[0]) + sum_rows_dot(slopes[2], q_heads[1])
         d_keys_1 = sum_rows_dot(slopes[1], q_heads[1])
-        g_k = weight_grad(3, jnp.concatenate([d_keys_0, d_keys_1], axis=0))
-        for half in range(2):
-            put(6 + half, 0, 16, g_k[:, half * 128 : half * 128 + 128])
-            streams[6 + half].scatter1()
+        put(KEYS, columns_in_halves(weight_grad(3, jnp.concatenate([d_keys_0, d_keys_1], axis=0))))
     with jax.named_scope("grads_q"):
         d_query_0 = rows_dot(heads_beside(slopes[0]), k_heads[0])
         d_query_1 = rows_dot(heads_beside(slopes[1]), k_heads[1]) + rows_dot(heads_beside(slopes[2]), k_heads[0])
-        g_q = weight_grad(2, jnp.concatenate([d_query_0, d_query_1], axis=0))
-        for half in range(2):
-            put(4 + half, 0, 16, g_q[:, half * 128 : half * 128 + 128])
-            streams[4 + half].scatter1()
+        put(QUERIES, columns_in_halves(weight_grad(2, jnp.concatenate([d_query_0, d_query_1], axis=0))))
     with jax.named_scope("scatter2_u"):
-        for s in streams[:2]:
+        for s in of(GATING):
             s.scatter2()
     with jax.named_scope("d_norm"):
         d_norm = cols_dot(dpre[0], w_own[0])
@@ -381,8 +361,8 @@
             d_norm = d_norm + cols_dot(dpre[g], w_own[g])
         dnorm[...] = d_norm.reshape(2, BLK, D)
         dnorm_copy = to_partner(dnorm.at[away], dnorm_in, 3)
-    with jax.named_scope("scatter2_v"):
-        for s in streams[2:4]:
+    with jax.named_scope("scatter2_out"):
+        for s in of(OUT):
             s.scatter2()
     with jax.named_scope("proj"):
         proj[...] = rows_dot(mixed, wo_own[...]).reshape(2, BLK, D)
@@ -404,15 +384,14 @@
         gain_copy = to_partner(gx0_own, gx0_own, 5)
 
     def gains_fan(axis, buf):
-        n, me = SIZES[axis], place.pos[axis]
-        own = buf.at[me]
-        for d in range(1, n):
+        own = buf.at[place.pos[axis]]
+        for _, device in place.peers[axis]:
             pltpu.make_async_remote_copy(
                 src_ref=own,
                 dst_ref=own,
                 send_sem=gssem.at[axis],
                 recv_sem=grsem.at[axis],
-                device_id=place.device(axis, lax.rem(me + d, n)),
+                device_id=device,
                 device_id_type=MESH,
             ).start()
 
@@ -424,11 +403,8 @@
             acc = acc + buf[j]
         return acc
 
-    with jax.named_scope("scatter2_k"):
-        for s in streams[6:]:
-            s.scatter2()
-    with jax.named_scope("scatter2_q"):
-        for s in streams[4:6]:
+    with jax.named_scope("scatter2_rest"):
+        for s in of(KEYS) + of(QUERIES) + of(VALUES):
             s.scatter2()
     with jax.named_scope("gains_x"):
         gain_copy.wait_recv()
@@ -444,35 +420,33 @@
         proj_copy.wait_recv()
         out_ref[...] = (hist[...].astype(F32) + valid_rows(core) * (proj[core] + proj_in[...])).astype(BF16)
 
-    with jax.named_scope("exchange_uv"):
-        for s in streams[:4]:
+    with jax.named_scope("exchange_first"):
+        for s in of(GATING) + of(OUT):
             s.exchange()
     with jax.named_scope("gains_y"):
         gx2[place.pos[1]] = gains_total(0, gx1)
         gains_fan(1, gx2)
-    with jax.named_scope("exchange_qk"):
-        for s in streams[4:]:
+    with jax.named_scope("exchange_rest"):
+        for s in of(KEYS) + of(VALUES) + of(QUERIES):
             s.exchange()
-    with jax.named_scope("gather2_uv"):
-        for s in streams[:4]:
+    with jax.named_scope("gather2_first"):
+        for s in of(GATING) + of(OUT):
             s.gather2()
     with jax.named_scope("gains_z"):
         gx3[place.pos[2]] = gains_total(1, gx2)
         gains_fan(2, gx3)
-    with jax.named_scope("gather2_qk"):
-        for s in streams[4:]:
+    with jax.named_scope("gather2_rest"):
+        for s in of(KEYS) + of(VALUES) + of(QUERIES):
             s.gather2()
-    with jax.named_scope("gather1_uv"):
-        for s in streams[:4]:
-            s.gather1()
-    with jax.named_scope("gather1_qk"):
-        for s in streams[4:]:
+    order = of(OUT) + of(GATING) + of(VALUES) + of(KEYS) + of(QUERIES)
+    with jax.named_scope("gather1"):
+        for s in order:
             s.gather1()
     with jax.named_scope("gains_end"):
         gains_ref[...] = gains_total(2, gx3)
     with jax.named_scope("finish"):
         forwards = []
-        for i, s in enumerate(streams):
+        for i, s in enumerate(order):
             s.finish()
             forwards.append(
                 pltpu.make_async_remote_copy(
@@ -511,7 +485,7 @@
 
     for half in range(2):
         for core in range(2):
-            part = wide(results[half][core, :, :, 16:32, :].reshape(D, 128))
+            part = wide(results[OUT + half][core].reshape(D, 128))
             for i in range(2):
                 column = (2 * half + i) * 128
                 w_out_wide[core * HALF : core * HALF + HALF, column : column + 128] = part[i * HALF : i * HALF + HALF]
@@ -520,7 +494,7 @@
         for core in range(2):
             for half in range(2):
                 column = (4 * g + 2 * core + half) * 128
-                part = results[2 * g + half][core, :, :, 0:16, :].reshape(D, 128)
+                part = results[STREAM_OF[g] + half][core].reshape(D, 128)
                 w_in_wide[:, column : column + 128] = wide(part)
             columns = slice((4 * g + 2 * core) * 128, (4 * g + 2 * core + 2) * 128)
             send(w_in_wide.at[:, columns], w_in_ref.at[:, columns])
@@ -552,15 +526,15 @@
     dma = pltpu.SemaphoreType.DMA
 
     buffers, result_shapes = [], []
-    for order, rows in STREAMS:
+    for order in STREAMS:
         n = [SIZES[a] for a in order]
-        result_shapes.append(shape((2, n[0], n[1], rows, 128), BF16))
+        result_shapes.append(shape((2, n[0], n[1], ROWS, 128), BF16))
         buffers += [
-            pltpu.VMEM((n[0], n[1], rows, 128), BF16),
-            pltpu.VMEM((n[0], n[1], rows, 128), BF16),
-            pltpu.VMEM((n[1], rows, 128), BF16),
-            pltpu.VMEM((n[1], rows, 128), BF16),
-            pltpu.VMEM((n[2], rows, 128), BF16),
+            pltpu.VMEM((n[0], n[1], ROWS, 128), BF16),
+            pltpu.VMEM((n[0], n[1], ROWS, 128), BF16),
+            pltpu.VMEM((n[1], ROWS, 128), BF16),
+            pltpu.VMEM((n[1], ROWS, 128), BF16),
+            pltpu.VMEM((n[2], ROWS, 128), BF16),
         ]
     ns = len(STREAMS)
     heads = pltpu.VMEM((2, HEADS * BLK, HALF), BF16)

time: 61.7 us -> 55.9 us (0.906)
  Pallas kernels: 60.2 us -> 54.5 us
    pallas_call x1, Pallas kernels: 57.6 us -> 51.8 us  [per_device(): pl.pallas_call(layer_kernel, out_shape=(shape((BLK, D), BF16), shape((BLK...]
where the time goes in v3:
time: 55.9 us; the launch traced here: 55.8 us
  Pallas kernels  54.5 us (97%)
  between operations  1.29 us (2%)
    pallas_call x1, Pallas kernels, per_device(): pl.pallas_call(layer_kernel, out_shape=(shape((BLK, D), BF16), shape((BLK...  51.8 us
    pallas_call x1, Pallas kernels, per_device(): pl.pallas_call(functools.partial(widen_kernel, factor), out_shape=(shape(...  2.64 us

profile of v3, /device:TPU:1, one launch (start us, length us, event | category | flops | bytes accessed | tf_op | source)
XLA Modules:
  0.0 55.8 jit_solution(7215147419569522359)
XLA Ops:
  1.3 51.8 %layer.1 = (bf16[128,512]{1,0:T(8,128)(2,1)S(1)}, bf16[128,512]{1,0:T(8,128)(2,1)S(1)}, f32[8,128]{1,0:T(8,128)S(1)}, bf16[2,4,8,16,128]{4,3,2,1,0:T(8,128)(2,1)...) custom-call(s32[1]{0:T(128)S(6)} %copy.13.len_ref, ...), custom_call_target="tpu_custom_call" | custom-call | tf_op jit(solution)/shard_map/layer/pallas_call | solution.py:541
  53.1 2.6 %widen.1 = (bf16[128,512]{1,0:T(8,128)(2,1)}, bf16[128,512]{1,0:T(8,128)(2,1)}, f32[512,2048]{1,0:T(8,128)}, f32[512,512]{1,0:T(8,128)}, f32[1,512]{1,0:T(1,128)}, /*index=5*/f32[1,512]{1,0:T(1,128)}) custom-call(bf16[128,512]{1,0:T(8,128)(2,1)S(1)} %get-tuple-element.25.refs_0_, bf16[128,512]{1,0:T(8,128)(2,1)S(1)} %get-tuple-element.26.refs_1_, ...), custom_call_target="tpu_custom_call" | custom-call | tf_op jit(solution)/shard_map/widen/pallas_call | solution.py:591

commit v4 on v3

--- a/solution.py
+++ b/solution.py
@@ -156,14 +156,21 @@
     (
         hist, gains, cots, normed, normed_t, xhat_own, w_own, wo_own, hid, slope, q_heads, k_heads, v_heads, d_heads,
         weights, turn, attended, dpre, stat_own, stat_other, proj, proj_in, dnorm, dnorm_in, gx0, gx1, gx2, gx3,
-        lsem, ssem, rsem, psem, qsem, gssem, grsem, fssem, frsem,
+        lsem, ssem, rsem, psem, qsem, gssem, grsem, fssem, frsem, relay,
     ) = rest
     place = Place()
     core = place.core
     away = 1 - core
     partner = place.partner
 
+    near = [device for axis in (1, 2) for _, device in place.peers[axis][3:]]
+    near += [device for _, device in place.peers[0]] + [partner]
+    two_away = [device for axis in (1, 2) for _, device in place.peers[axis][3:5]]
+
     with jax.named_scope("start"):
+        barrier = pltpu.get_barrier_semaphore()
+        for device in near:
+            pl.semaphore_signal(barrier, inc=1, device_id=device, device_id_type=MESH)
         first = pl.multiple_of(core * HALF, HALF)
         loads = [
             pltpu.make_async_copy(hist_hbm, hist, lsem.at[0]),
@@ -180,12 +187,6 @@
         loads += [wo_load, ga_load]
         for load in loads:
             load.start()
-
-        barrier = pltpu.get_barrier_semaphore()
-        pl.semaphore_signal(barrier, inc=1, device_id=partner, device_id_type=MESH)
-        for peers in place.peers:
-            for _, device in peers:
-                pl.semaphore_signal(barrier, inc=1, device_id=device, device_id_type=MESH)
 
     streams = [
         Stream(place, order, stream_bufs[5 * i : 5 * i + 5], results[i].at[core], ssem, rsem, LEVELS * i)
@@ -261,9 +262,11 @@
         project(core, True)
     with jax.named_scope("barrier"):
         loads[2].wait()
-        pl.semaphore_wait(barrier, 18)
+        pl.semaphore_wait(barrier, len(near))
         normed_copy = to_partner(normed.at[core], normed.at[core], 0)
         cots_copy = to_partner(cots.at[core], cots.at[core], 1)
+        for device in two_away:
+            pl.semaphore_signal(relay, inc=1, device_id=device, device_id_type=MESH)
     with jax.named_scope("own_attend"):
         attended[core] = attend(core, core, core, True)
     with jax.named_scope("share_wait"):
@@ -333,6 +336,7 @@
     with jax.named_scope("grads_u"):
         put(GATING, columns_in_halves(weight_grad(0, d_mixed * ng)))
         g_out = rows_dot(mixed.T, d_proj)
+        pl.semaphore_wait(relay, len(two_away))
         g_out = [g_out[:, i * 128 : i * 128 + 128] for i in range(4)]
         put(OUT, [jnp.concatenate(g_out[:2], axis=0), jnp.concatenate(g_out[2:], axis=0)])
     with jax.named_scope("grads_v"):
@@ -423,21 +427,21 @@
     with jax.named_scope("exchange_first"):
         for s in of(GATING) + of(OUT):
             s.exchange()
+    with jax.named_scope("exchange_rest"):
+        for s in of(KEYS) + of(VALUES) + of(QUERIES):
+            s.exchange()
     with jax.named_scope("gains_y"):
         gx2[place.pos[1]] = gains_total(0, gx1)
         gains_fan(1, gx2)
-    with jax.named_scope("exchange_rest"):
-        for s in of(KEYS) + of(VALUES) + of(QUERIES):
-            s.exchange()
     with jax.named_scope("gather2_first"):
         for s in of(GATING) + of(OUT):
+            s.gather2()
+    with jax.named_scope("gather2_rest"):
+        for s in of(KEYS) + of(VALUES) + of(QUERIES):
             s.gather2()
     with jax.named_scope("gains_z"):
         gx3[place.pos[2]] = gains_total(1, gx2)
         gains_fan(2, gx3)
-    with jax.named_scope("gather2_rest"):
-        for s in of(KEYS) + of(VALUES) + of(QUERIES):
-            s.gather2()
     order = of(OUT) + of(GATING) + of(VALUES) + of(KEYS) + of(QUERIES)
     with jax.named_scope("gather1"):
         for s in order:
@@ -582,6 +586,7 @@
             dma((3,)),
             dma((ns,)),
             dma((ns,)),
+            pltpu.SemaphoreType.REGULAR,
         ],
         compiler_params=pltpu.CompilerParams(collective_id=1, has_side_effects=True, vmem_limit_bytes=48 << 20),
         name="layer",

time: 55.9 us -> 54.9 us (0.982)
  Pallas kernels: 54.5 us -> 53.5 us
    pallas_call x1, Pallas kernels: 51.8 us -> 50.8 us  [per_device(): pl.pallas_call(layer_kernel, out_shape=(shape((BLK, D), BF16), shape((BLK...]
where the time goes in v4:
time: 54.9 us; the launch traced here: 54.7 us
  Pallas kernels  53.5 us (97%)
  between operations  1.29 us (2%)
    pallas_call x1, Pallas kernels, per_device(): pl.pallas_call(layer_kernel, out_shape=(shape((BLK, D), BF16), shape((BLK...  50.8 us
    pallas_call x1, Pallas kernels, per_device(): pl.pallas_call(functools.partial(widen_kernel, factor), out_shape=(shape(...  2.64 us

profile of v4, /device:TPU:1, one launch (start us, length us, event | category | flops | bytes accessed | tf_op | source)
XLA Modules:
  0.0 54.7 jit_solution(18147126426086899787)
XLA Ops:
  1.3 50.8 %layer.1 = (bf16[128,512]{1,0:T(8,128)(2,1)S(1)}, bf16[128,512]{1,0:T(8,128)(2,1)S(1)}, f32[8,128]{1,0:T(8,128)S(1)}, bf16[2,4,8,16,128]{4,3,2,1,0:T(8,128)(2,1)...) custom-call(s32[1]{0:T(128)S(6)} %copy.13.len_ref, ...), custom_call_target="tpu_custom_call" | custom-call | tf_op jit(solution)/shard_map/layer/pallas_call | solution.py:545
  52.1 2.6 %widen.1 = (bf16[128,512]{1,0:T(8,128)(2,1)}, bf16[128,512]{1,0:T(8,128)(2,1)}, f32[512,2048]{1,0:T(8,128)}, f32[512,512]{1,0:T(8,128)}, f32[1,512]{1,0:T(1,128)}, /*index=5*/f32[1,512]{1,0:T(1,128)}) custom-call(bf16[128,512]{1,0:T(8,128)(2,1)S(1)} %get-tuple-element.25.refs_0_, bf16[128,512]{1,0:T(8,128)(2,1)S(1)} %get-tuple-element.26.refs_1_, ...), custom_call_target="tpu_custom_call" | custom-call | tf_op jit(solution)/shard_map/widen/pallas_call | solution.py:596

commit v5 on v4

--- a/solution.py
+++ b/solution.py
@@ -356,22 +356,40 @@
         d_query_0 = rows_dot(heads_beside(slopes[0]), k_heads[0])
         d_query_1 = rows_dot(heads_beside(slopes[1]), k_heads[1]) + rows_dot(heads_beside(slopes[2]), k_heads[0])
         put(QUERIES, columns_in_halves(weight_grad(2, jnp.concatenate([d_query_0, d_query_1], axis=0))))
-    with jax.named_scope("scatter2_u"):
-        for s in of(GATING):
-            s.scatter2()
+    def gains_fan(axis, buf):
+        own = buf.at[place.pos[axis]]
+        for _, device in place.peers[axis]:
+            pltpu.make_async_remote_copy(
+                src_ref=own,
+                dst_ref=own,
+                send_sem=gssem.at[axis],
+                recv_sem=grsem.at[axis],
+                device_id=device,
+                device_id_type=MESH,
+            ).start()
+
+    def gains_total(axis, buf):
+        n = SIZES[axis]
+        wait_bytes(buf.at[pl.ds(0, n - 1)], grsem.at[axis])
+        acc = buf[0]
+        for j in range(1, n):
+            acc = acc + buf[j]
+        return acc
+
+    order = of(OUT) + of(GATING) + of(VALUES) + of(KEYS) + of(QUERIES)
     with jax.named_scope("d_norm"):
         d_norm = cols_dot(dpre[0], w_own[0])
         for g in range(1, 4):
             d_norm = d_norm + cols_dot(dpre[g], w_own[g])
         dnorm[...] = d_norm.reshape(2, BLK, D)
         dnorm_copy = to_partner(dnorm.at[away], dnorm_in, 3)
-    with jax.named_scope("scatter2_out"):
-        for s in of(OUT):
-            s.scatter2()
     with jax.named_scope("proj"):
         proj[...] = rows_dot(mixed, wo_own[...]).reshape(2, BLK, D)
         proj_copy = to_partner(proj.at[away], proj_in, 4)
 
+    with jax.named_scope("scatter2_u"):
+        for s in of(GATING):
+            s.scatter2()
     with jax.named_scope("gain_sums"):
         xhat = xhat_own[...]
         dnorm_copy.wait_recv()
@@ -387,34 +405,6 @@
             gx0_own[6 + i : 7 + i, :] = part * (1.0 - mine)
         gain_copy = to_partner(gx0_own, gx0_own, 5)
 
-    def gains_fan(axis, buf):
-        own = buf.at[place.pos[axis]]
-        for _, device in place.peers[axis]:
-            pltpu.make_async_remote_copy(
-                src_ref=own,
-                dst_ref=own,
-                send_sem=gssem.at[axis],
-                recv_sem=grsem.at[axis],
-                device_id=device,
-                device_id_type=MESH,
-            ).start()
-
-    def gains_total(axis, buf):
-        n = SIZES[axis]
-        wait_bytes(buf.at[pl.ds(0, n - 1)], grsem.at[axis])
-        acc = buf[0]
-        for j in range(1, n):
-            acc = acc + buf[j]
-        return acc
-
-    with jax.named_scope("scatter2_rest"):
-        for s in of(KEYS) + of(QUERIES) + of(VALUES):
-            s.scatter2()
-    with jax.named_scope("gains_x"):
-        gain_copy.wait_recv()
-        gx1[place.pos[0]] = gx0[0] + gx0[1]
-        gains_fan(0, gx1)
-
     with jax.named_scope("grad_history"):
         e = d_norm * gains[0]
         d_hist = rstd_in * (
@@ -424,30 +414,38 @@
         proj_copy.wait_recv()
         out_ref[...] = (hist[...].astype(F32) + valid_rows(core) * (proj[core] + proj_in[...])).astype(BF16)
 
+    with jax.named_scope("scatter2_out"):
+        for s in of(OUT):
+            s.scatter2()
+    with jax.named_scope("gains_x"):
+        gain_copy.wait_recv()
+        gx1[place.pos[0]] = gx0[0] + gx0[1]
+        gains_fan(0, gx1)
+
+    with jax.named_scope("scatter2_rest"):
+        for s in of(KEYS) + of(QUERIES) + of(VALUES):
+            s.scatter2()
     with jax.named_scope("exchange_first"):
         for s in of(GATING) + of(OUT):
-            s.exchange()
-    with jax.named_scope("exchange_rest"):
-        for s in of(KEYS) + of(VALUES) + of(QUERIES):
             s.exchange()
     with jax.named_scope("gains_y"):
         gx2[place.pos[1]] = gains_total(0, gx1)
         gains_fan(1, gx2)
+    with jax.named_scope("exchange_rest"):
+        for s in of(KEYS) + of(VALUES) + of(QUERIES):
+            s.exchange()
     with jax.named_scope("gather2_first"):
         for s in of(GATING) + of(OUT):
-            s.gather2()
-    with jax.named_scope("gather2_rest"):
-        for s in of(KEYS) + of(VALUES) + of(QUERIES):
             s.gather2()
     with jax.named_scope("gains_z"):
         gx3[place.pos[2]] = gains_total(1, gx2)
         gains_fan(2, gx3)
-    order = of(OUT) + of(GATING) + of(VALUES) + of(KEYS) + of(QUERIES)
+    with jax.named_scope("gather2_rest"):
+        for s in of(KEYS) + of(VALUES) + of(QUERIES):
+            s.gather2()
     with jax.named_scope("gather1"):
         for s in order:
             s.gather1()
-    with jax.named_scope("gains_end"):
-        gains_ref[...] = gains_total(2, gx3)
     with jax.named_scope("finish"):
         forwards = []
         for i, s in enumerate(order):
@@ -463,6 +461,8 @@
                 )
             )
             forwards[-1].start()
+    with jax.named_scope("gains_end"):
+        gains_ref[...] = gains_total(2, gx3)
     with jax.named_scope("drain"):
         for axis, buf in enumerate((gx1, gx2, gx3)):
             wait_bytes(buf.at[pl.ds(0, SIZES[axis] - 1)], gssem.at[axis])

time: 54.9 us -> 54.2 us (0.987)
  Pallas kernels: 53.5 us -> 52.7 us
    pallas_call x1, Pallas kernels: 50.8 us -> 50.1 us  [per_device(): pl.pallas_call(layer_kernel, out_shape=(shape((BLK, D), BF16), shape((BLK...]
where the time goes in v5:
time: 54.2 us; the launch traced here: 54 us
  Pallas kernels  52.7 us (97%)
  between operations  1.29 us (2%)
    pallas_call x1, Pallas kernels, per_device(): pl.pallas_call(layer_kernel, out_shape=(shape((BLK, D), BF16), shape((BLK...  50.1 us
    pallas_call x1, Pallas kernels, per_device(): pl.pallas_call(functools.partial(widen_kernel, factor), out_shape=(shape(...  2.64 us

profile of v5, /device:TPU:1, one launch (start us, length us, event | category | flops | bytes accessed | tf_op | source)
XLA Modules:
  0.0 54.0 jit_solution(7726745221263585239)
XLA Ops:
  1.3 50.1 %layer.1 = (bf16[128,512]{1,0:T(8,128)(2,1)S(1)}, bf16[128,512]{1,0:T(8,128)(2,1)S(1)}, f32[8,128]{1,0:T(8,128)S(1)}, bf16[2,4,8,16,128]{4,3,2,1,0:T(8,128)(2,1)...) custom-call(s32[1]{0:T(128)S(6)} %copy.13.len_ref, ...), custom_call_target="tpu_custom_call" | custom-call | tf_op jit(solution)/shard_map/layer/pallas_call | solution.py:545
  51.4 2.6 %widen.1 = (bf16[128,512]{1,0:T(8,128)(2,1)}, bf16[128,512]{1,0:T(8,128)(2,1)}, f32[512,2048]{1,0:T(8,128)}, f32[512,512]{1,0:T(8,128)}, f32[1,512]{1,0:T(1,128)}, /*index=5*/f32[1,512]{1,0:T(1,128)}) custom-call(bf16[128,512]{1,0:T(8,128)(2,1)S(1)} %get-tuple-element.25.refs_0_, bf16[128,512]{1,0:T(8,128)(2,1)S(1)} %get-tuple-element.26.refs_1_, ...), custom_call_target="tpu_custom_call" | custom-call | tf_op jit(solution)/shard_map/widen/pallas_call | solution.py:596

commit v6 on v5

--- a/solution.py
+++ b/solution.py
@@ -155,7 +155,7 @@
     stream_bufs, rest = rest[: 5 * ns], rest[5 * ns :]
     (
         hist, gains, cots, normed, normed_t, xhat_own, w_own, wo_own, hid, slope, q_heads, k_heads, v_heads, d_heads,
-        weights, turn, attended, dpre, stat_own, stat_other, proj, proj_in, dnorm, dnorm_in, gx0, gx1, gx2, gx3,
+        weights, turn, attended, d_proj, d_mix, dpre, stat_own, stat_other, proj, proj_in, dnorm, dnorm_in, gx0, gx1, gx2, gx3,
         lsem, ssem, rsem, psem, qsem, gssem, grsem, fssem, frsem, relay,
     ) = rest
     place = Place()
@@ -253,6 +253,11 @@
         turn[tile] = turned
         return rows_dot(heads_beside(weight), v_heads[k_block])
 
+    def back_through_out(block):
+        d_out = (cots[block].astype(F32) * valid_rows(block)).astype(BF16)
+        d_proj[block] = d_out
+        d_mix[block] = cols_dot(d_out, wo_own[...])
+
     with jax.named_scope("own_project"):
         loads[0].wait()
         loads[1].wait()
@@ -269,6 +274,11 @@
             pl.semaphore_signal(relay, inc=1, device_id=device, device_id_type=MESH)
     with jax.named_scope("own_attend"):
         attended[core] = attend(core, core, core, True)
+    with jax.named_scope("own_mixed"):
+        wo_load.wait()
+        ga_load.wait()
+        gain_attn = gains[1, :, pl.ds(first, HALF)]
+        back_through_out(core)
     with jax.named_scope("share_wait"):
         normed_copy.wait_recv()
     with jax.named_scope("other_project"):
@@ -276,16 +286,13 @@
     with jax.named_scope("other_attend"):
         attended[away] = attend(away, away, away, True)
         attended[1] = attended[1] + attend(2, 1, 0, False)
-    with jax.named_scope("d_mixed"):
+    with jax.named_scope("other_mixed"):
         cots_copy.wait_recv()
-        wo_load.wait()
-        ga_load.wait()
+        back_through_out(away)
         valid = jnp.concatenate([valid_rows(0), valid_rows(1)], axis=0)
-        d_proj = (cots[...].reshape(SEQ, D).astype(F32) * valid).astype(BF16)
-        gain_attn = gains[1, :, pl.ds(first, HALF)]
         att = attended[...].reshape(SEQ, HALF) * valid
         gating = hid[0].reshape(SEQ, HALF).astype(F32)
-        d_mixed = cols_dot(d_proj, wo_own[...])
+        d_mixed = d_mix[...].reshape(SEQ, HALF)
         g = d_mixed * gain_attn * gating
     with jax.named_scope("stats"):
         half_mean = jnp.mean(att, axis=-1, keepdims=True)
@@ -335,7 +342,7 @@
 
     with jax.named_scope("grads_u"):
         put(GATING, columns_in_halves(weight_grad(0, d_mixed * ng)))
-        g_out = rows_dot(mixed.T, d_proj)
+        g_out = rows_dot(mixed.T, d_proj[...].reshape(SEQ, D))
         pl.semaphore_wait(relay, len(two_away))
         g_out = [g_out[:, i * 128 : i * 128 + 128] for i in range(4)]
         put(OUT, [jnp.concatenate(g_out[:2], axis=0), jnp.concatenate(g_out[2:], axis=0)])
@@ -566,6 +573,8 @@
             pltpu.VMEM((3, HEADS * BLK, BLK), BF16),
             pltpu.VMEM((3, HEADS * BLK, BLK), F32),
             pltpu.VMEM((2, BLK, HALF), F32),
+            pltpu.VMEM((2, BLK, D), BF16),
+            pltpu.VMEM((2, BLK, HALF), F32),
             pltpu.VMEM((4, SEQ, HALF), BF16),
             pltpu.VMEM((SEQ, 128), F32),
             pltpu.VMEM((SEQ, 128), F32),

time: 54.2 us -> 54.7 us (level)
  Pallas kernels: 52.7 us -> 53.3 us
where the time goes in v6:
time: 54.7 us; the launch traced here: 54.5 us
  Pallas kernels  53.3 us (97%)
  between operations  1.29 us (2%)
    pallas_call x1, Pallas kernels, per_device(): pl.pallas_call(layer_kernel, out_shape=(shape((BLK, D), BF16), shape((BLK...  50.6 us
    pallas_call x1, Pallas kernels, per_device(): pl.pallas_call(functools.partial(widen_kernel, factor), out_shape=(shape(...  2.64 us

profile of v6, /device:TPU:1, one launch (start us, length us, event | category | flops | bytes accessed | tf_op | source)
XLA Modules:
  0.0 54.5 jit_solution(13869410378894838041)
XLA Ops:
  1.3 50.6 %layer.1 = (bf16[128,512]{1,0:T(8,128)(2,1)S(1)}, bf16[128,512]{1,0:T(8,128)(2,1)S(1)}, f32[8,128]{1,0:T(8,128)S(1)}, bf16[2,4,8,16,128]{4,3,2,1,0:T(8,128)(2,1)...) custom-call(s32[1]{0:T(128)S(6)} %copy.13.len_ref, ...), custom_call_target="tpu_custom_call" | custom-call | tf_op jit(solution)/shard_map/layer/pallas_call | solution.py:552
  51.9 2.6 %widen.1 = (bf16[128,512]{1,0:T(8,128)(2,1)}, bf16[128,512]{1,0:T(8,128)(2,1)}, f32[512,2048]{1,0:T(8,128)}, f32[512,512]{1,0:T(8,128)}, f32[1,512]{1,0:T(1,128)}, /*index=5*/f32[1,512]{1,0:T(1,128)}) custom-call(bf16[128,512]{1,0:T(8,128)(2,1)S(1)} %get-tuple-element.25.refs_0_, bf16[128,512]{1,0:T(8,128)(2,1)S(1)} %get-tuple-element.26.refs_1_, ...), custom_call_target="tpu_custom_call" | custom-call | tf_op jit(solution)/shard_map/widen/pallas_call | solution.py:605
